TPU v7x, 32 devices: a whole 2x2x4 slice. The times are simulated.
32 devices in a mesh: ctx: 16 (over z, y, core), head: 2 (over x).
Axes of the slice: x: 2, y: 2, z: 4, core: 2. Of those that a mesh axis runs over, the one named last changes fastest.
Arguments:
- queries: bfloat16 [2048, 16, 128], P('ctx', 'head'), may hold values from -30 to 30
- rotated_keys: bfloat16 [2048, 8, 128], P('ctx', 'head'), may hold values from -4 to 4
- value_vectors: bfloat16 [2048, 8, 128], P('ctx', 'head'), may hold values from -6 to 6
- out_grad: bfloat16 [2048, 5376], P('ctx', 'head'), may hold values from -6 to 6
- out_proj: bfloat16 [5376, 2048], P('ctx', 'head'), may hold values from -0.125 to 0.125
- seg_ids: int32 [2048], replicated, may hold values from 0 to 3, never falling along the last dimension, each value on 1 to 1024 neighbouring positions
Outputs:
- layer_out: bfloat16 [2048, 5376], P('ctx', 'head')
- query_gradient: bfloat16 [2048, 16, 128], P('ctx', 'head')
- grad_key: bfloat16 [2048, 8, 128], P('ctx', 'head')
- grad_value: bfloat16 [2048, 8, 128], P('ctx', 'head')
- grad_proj: float32 [5376, 2048], P('ctx', 'head')
Inputs may be any that keep to these rules, and one draw needn't show every extreme that they name: `seg_ids`: segment ids never fall along the slab; every one of the 4 books holds one token or more.
All inputs are finite; a program needn't handle non-finite values.
Results may differ from a plain program's by a relative error of at most 0.025.
Values may be sent and summed in bfloat16 or wider, within the bound.
A program may use at most 128 MiB of HBM per device.

v0:
```python
import jax
import jax.numpy as jnp
from jax import lax
from jax.sharding import PartitionSpec as P

WINDOW_TOKENS = 1024


def passed_along(value, axis, by):
    count = lax.axis_size(axis)
    pairs = [(i, i + by) for i in range(count) if 0 <= i + by < count]
    return lax.ppermute(value, axis, pairs)


def shards(queries, rotated_keys, value_vectors, out_grad, out_proj, seg_ids):
    logit_scale = 168.0 ** (-0.5)
    tok_rows = queries.shape[0]
    heads_query = queries.shape[1]
    heads_kv = rotated_keys.shape[1]
    head_size = queries.shape[2]
    group_size = heads_query // heads_kv
    blocks = WINDOW_TOKENS // tok_rows
    ctx_count = lax.axis_size("ctx")
    ctx_index = lax.axis_index("ctx")
    own_block = jnp.stack([rotated_keys, value_vectors])
    received = []
    for offset in range(blocks):
        received.append(passed_along(own_block, "ctx", offset + 1))
    key_value = jnp.concatenate(received[::-1] + [own_block], axis=1)
    key_row_slice = key_value[0]
    value_row_slice = key_value[1]
    first_row = ctx_index * tok_rows
    seg_padded = jnp.concatenate([jnp.full((WINDOW_TOKENS,), -1, jnp.int32), seg_ids], 0)
    key_seg = lax.dynamic_slice_in_dim(seg_padded, first_row, WINDOW_TOKENS + tok_rows, 0)
    query_seg = lax.dynamic_slice_in_dim(seg_ids, first_row, tok_rows, 0)
    query_pos = first_row + jnp.arange(tok_rows, dtype=jnp.int32)
    key_pos = first_row - WINDOW_TOKENS + jnp.arange(WINDOW_TOKENS + tok_rows, dtype=jnp.int32)
    allowed = (key_pos[None, :] <= query_pos[:, None]) & (
        query_pos[:, None] - key_pos[None, :] < WINDOW_TOKENS
    )
    allowed = allowed & (key_pos[None, :] >= 0) & (query_seg[:, None] == key_seg[None, :])
    grouped_queries = queries.reshape(tok_rows, heads_kv, group_size, head_size)
    attention_logits = logit_scale * jnp.einsum(
        "eqco,fqo->qcef", grouped_queries, key_row_slice, preferred_element_type=jnp.float32
    )
    attention_logits = jnp.where(allowed, attention_logits, -1e30)
    top_score = jnp.max(attention_logits, axis=3, keepdims=True)
    weights = jnp.where(allowed, jnp.exp(attention_logits - top_score), 0.0)
    probs = weights / jnp.sum(weights, axis=3, keepdims=True)
    probabilities_half = probs.astype(jnp.bfloat16)
    attended_output = jnp.einsum(
        "ykip,pyj->iykj", probabilities_half, value_row_slice, preferred_element_type=jnp.float32
    )
    attended_output = attended_output.astype(jnp.bfloat16).reshape(
        tok_rows, heads_query * head_size
    )
    proj_full = lax.all_gather(out_proj, "ctx", axis=0, tiled=True)
    out_partial = lax.dot_general(
        attended_output, proj_full, (((1,), (1,)), ((), ())), preferred_element_type=jnp.float32
    )
    layer_out = lax.psum_scatter(out_partial, "head", scatter_dimension=1, tiled=True).astype(
        jnp.bfloat16
    )
    grad_full = lax.all_gather(out_grad, "head", axis=1, tiled=True)
    grad_attended = jnp.dot(grad_full, proj_full, preferred_element_type=jnp.float32).astype(
        jnp.bfloat16
    )
    proj_summed = lax.psum_scatter(
        lax.dot_general(
            grad_full, attended_output, (((0,), (0,)), ((), ())), preferred_element_type=jnp.float32
        ),
        "ctx",
        scatter_dimension=0,
        tiled=True,
    )
    grad_proj = proj_summed * (ctx_count * tok_rows) ** (-0.5)
    grouped_gradient = grad_attended.reshape(tok_rows, heads_kv, group_size, head_size)
    attn_groups = attended_output.reshape(tok_rows, heads_kv, group_size, head_size)
    probability_gradient = jnp.einsum(
        "eqco,fqo->qcef", grouped_gradient, value_row_slice, preferred_element_type=jnp.float32
    )
    row_delta = jnp.sum(
        grouped_gradient.astype(jnp.float32) * attn_groups.astype(jnp.float32), axis=3
    )
    row_delta = jnp.transpose(row_delta, (1, 2, 0))[..., None]
    score_gradient = (probs * (probability_gradient - row_delta)).astype(jnp.bfloat16)
    query_gradient = logit_scale * jnp.einsum(
        "ykip,pyj->iykj", score_gradient, key_row_slice, preferred_element_type=jnp.float32
    )
    query_gradient = query_gradient.astype(jnp.bfloat16).reshape(tok_rows, heads_query, head_size)
    key_portion = logit_scale * jnp.einsum(
        "huoe,ohul->ehl", score_gradient, grouped_queries, preferred_element_type=jnp.float32
    )
    value_portion = jnp.einsum(
        "huoe,ohul->ehl", probabilities_half, grouped_gradient, preferred_element_type=jnp.float32
    )
    both_parts = jnp.stack([key_portion, value_portion])
    halo_part = both_parts[:, :WINDOW_TOKENS]
    summed = both_parts[:, WINDOW_TOKENS:]
    for offset in range(blocks):
        distance = offset + 1
        portion = halo_part[:, (blocks - distance) * tok_rows : (blocks - distance + 1) * tok_rows]
        summed = summed + passed_along(portion, "ctx", -distance)
    grad_key = summed[0].astype(jnp.bfloat16)
    grad_value = summed[1].astype(jnp.bfloat16)
    return (layer_out, query_gradient, grad_key, grad_value, grad_proj)


def solution(mesh):
    return jax.shard_map(
        shards,
        mesh=mesh,
        in_specs=(
            P("ctx", "head", None),
            P("ctx", "head", None),
            P("ctx", "head", None),
            P("ctx", "head"),
            P("ctx", "head"),
            P(),
        ),
        out_specs=(
            P("ctx", "head"),
            P("ctx", "head", None),
            P("ctx", "head", None),
            P("ctx", "head", None),
            P("ctx", "head"),
        ),
        check_vma=False,
    )
```

profile of v0, /device:TPU:0, one launch (start us, length us, event | category | flops | bytes accessed | tf_op | source)
XLA Modules:
  0.0 526.7 jit_solution(9161043256023241534)
XLA Ops:
  8.7 1.0 copy_bitcast_fusion
  9.8 2.4 collective-permute-start.7
  12.1 4.4 collective-permute-start.6
  16.6 4.4 collective-permute-start.2
  21.0 3.9 collective-permute-start.1
  24.9 1.3 collective-permute-start
  26.4 1.0 fusion.13
  27.5 11.3 %collective-permute-done = bf16[2,128,4,128]{3,1,2,0:T(8,128)(2,1)S(1)} collective-permute-done((bf16[2,128,4,128]{3,1,2,0:T(8,128)(2,1)S(1)}, bf16[2,128,4,128]{3,1,2,0:T(8,128)(2,1)S(1)}, u32[]{:S(2)}, u32[]{:S(2)}) %collective-permute-start) | collective-permute-done | bytes 262176 | tf_op jit(solution)/shard_map/ppermute | solution.py:12
  38.7 11.9 %collective-permute-start.3 = (bf16[2,128,4,128]{3,1,2,0:T(8,128)(2,1)S(1)}, bf16[2,128,4,128]{3,1,2,0:T(8,128)(2,1)S(1)}, u32[]{:S(2)}, u32[]{:S(2)}) collective-permute-start(bf16[2,128,4,128]{3,1,2,0:T(8,128)(2,1)S(1)} %pad_maximum_fusion.1), channel_id=1, source_target_pairs={{0,10},{2,12},{4,14},{6,16},{8,18},{10,20},{12,22},{14,24},{16,26}... | collective-permute-start | bytes 786440 | tf_op jit(solution)/shard_map/ppermute | solution.py:12
  50.7 1.3 collective-permute-start.4
  52.0 38.6 %collective-permute-start.5 = (bf16[2,128,4,128]{3,1,2,0:T(8,128)(2,1)S(1)}, bf16[2,128,4,128]{3,1,2,0:T(8,128)(2,1)S(1)}, u32[]{:S(2)}, u32[]{:S(2)}) collective-permute-start(bf16[2,128,4,128]{3,1,2,0:T(8,128)(2,1)S(1)} %pad_maximum_fusion.1), channel_id=1, source_target_pairs={{0,6},{2,8},{4,10},{6,12},{8,14},{10,16},{12,18},{14,20},{16,22},{... | collective-permute-start | bytes 786440 | tf_op jit(solution)/shard_map/ppermute | solution.py:12
  90.8 9.3 %collective-permute-done.5 = bf16[2,128,4,128]{3,1,2,0:T(8,128)(2,1)S(1)} collective-permute-done((bf16[2,128,4,128]{3,1,2,0:T(8,128)(2,1)S(1)}, bf16[2,128,4,128]{3,1,2,0:T(8,128)(2,1)S(1)}, u32[]{:S(2)}, u32[]{:S(2)}) %collective-permute-start.5) | collective-permute-done | bytes 262176 | tf_op jit(solution)/shard_map/ppermute | solution.py:12
  100.2 1.4 copy-done.5
  101.7 5.4 %fusion.41 = (f32[4,2,128]{2,1,0:T(2,128)S(1)}, f32[4,2,128,1152]{2,3,1,0:T(8,128)}) fusion(pred[128,1152]{0,1:T(8,128)(4,1)S(1)} %fusion.13, bf16[128,4,2,128]{3,2,1,0:T(2,128)(2,1)S(1)} %bitcast.98, bf16[2,1152,4,128]{3,1,2,0:T(8,128)(2,1)} %copy-done.5), kind=kOutput, calls=%fused_computation.86 | convolution fusion | flops 307889280 | bytes 6459392 | tf_op jit(solution)/shard_map/sub | solution.py:48
  107.1 2.8 fusion.9
  110.0 33.8 %all-gather.3.cloned.1.call-done = bf16[5376,1024]{1,0:T(8,128)(2,1)} async-done(((bf16[336,1024]{1,0:T(8,128)(2,1)}), bf16[5376,1024]{1,0:T(8,128)(2,1)}) %all-gather.3.cloned.1.call-update) | async-done | bytes 11010064 | tf_op jit(solution)/shard_map/all_gather | solution.py:57
  143.8 6.1 %convolution_convert_fusion.1 = bf16[128,1024]{1,0:T(8,128)(2,1)S(1)} fusion(bf16[128,5376]{1,0:T(8,128)(2,1)} %all-gather.5.cloned.1.call-done, bf16[5376,1024]{1,0:T(8,128)(2,1)} %all-gather.3.cloned.1.call-done), kind=kOutput, calls=%fused_computation.37 | convolution fusion | flops 1409417216 | bytes 12648448 | tf_op jit(solution)/shard_map/dot_general | solution.py:65
  150.2 1.9 multiply_reduce_fusion
  152.1 9.4 %fusion.44 = f32[128,5376]{1,0:T(8,128)} fusion(bf16[128,1024]{0,1:T(8,128)(2,1)S(1)} %bitcast.100, bf16[5376,1024]{1,0:T(8,128)(2,1)} %all-gather.3.cloned.1.call-done), kind=kOutput, calls=%fused_computation.87 | convolution fusion | flops 1409286144 | bytes 14024704 | tf_op jit(solution)/shard_map/dot_general | solution.py:58
  161.7 1.1 copy-done.2
  162.8 9.0 %convolution_bitcast_fusion = f32[5376,1024]{0,1:T(8,128)} fusion(bf16[128,1024]{0,1:T(8,128)(2,1)S(1)} %bitcast.101, bf16[128,5376]{1,0:T(8,128)(2,1)S(1)} %copy-done.2), kind=kOutput, calls=%fused_computation.1 | convolution fusion | flops 1409286144 | bytes 23658496 | tf_op jit(solution)/shard_map/dot_general | solution.py:69
  171.8 21.9 %copy.58 = f32[5376,1024]{1,0:T(8,128)} copy(f32[5376,1024]{0,1:T(8,128)} %convolution_bitcast_fusion) | data formatting | bytes 44040192
  193.7 1.6 copy-done.6
  195.3 3.2 fusion.3
  198.5 0.8 fusion.6
  199.3 0.9 copy-done.4
  200.2 0.8 convolution_bitcast_fusion.1
  200.9 1.5 fusion.24
  202.5 0.9 copy-done.1
  203.4 1.3 collective-permute-start.8
  204.7 1.3 collective-permute-start.9
  206.0 1.3 collective-permute-start.10
  207.3 1.3 collective-permute-start.11
  208.6 1.3 collective-permute-start.12
  209.9 1.3 collective-permute-start.13
  211.2 19.4 %collective-permute-done.9 = f32[2,128,4,128]{3,1,2,0:T(8,128)} collective-permute-done((f32[2,128,4,128]{3,1,2,0:T(8,128)S(1)}, f32[2,128,4,128]{3,1,2,0:T(8,128)}, u32[]{:S(2)}, u32[]{:S(2)}) %collective-permute-start.9) | collective-permute-done | bytes 524320 | tf_op jit(solution)/shard_map/ppermute | solution.py:12
  230.6 1.3 collective-permute-start.15
  232.4 1.3 collective-permute-start.14
  234.3 0.9 copy.39
  235.2 18.9 %collective-permute-done.11 = f32[2,128,4,128]{3,1,2,0:T(8,128)} collective-permute-done((f32[2,128,4,128]{3,1,2,0:T(8,128)}, f32[2,128,4,128]{3,1,2,0:T(8,128)}, u32[]{:S(2)}, u32[]{:S(2)}) %collective-permute-start.11) | collective-permute-done | bytes 524320 | tf_op jit(solution)/shard_map/ppermute | solution.py:12
  254.1 4.8 collective-permute-done.12
  258.9 13.0 %collective-permute-done.13 = f32[2,128,4,128]{3,1,2,0:T(8,128)} collective-permute-done((f32[2,128,4,128]{3,1,2,0:T(8,128)}, f32[2,128,4,128]{3,1,2,0:T(8,128)}, u32[]{:S(2)}, u32[]{:S(2)}) %collective-permute-start.13) | collective-permute-done | bytes 524320 | tf_op jit(solution)/shard_map/ppermute | solution.py:12
  271.9 140.8 %collective-permute-done.15 = f32[2,128,4,128]{3,1,2,0:T(8,128)} collective-permute-done((f32[2,128,4,128]{3,1,2,0:T(8,128)}, f32[2,128,4,128]{3,1,2,0:T(8,128)}, u32[]{:S(2)}, u32[]{:S(2)}) %collective-permute-start.15) | collective-permute-done | bytes 524320 | tf_op jit(solution)/shard_map/ppermute | solution.py:12
  412.6 2.4 fusion.30
  416.6 2.3 convert_element_type.41
  418.8 97.8 %reduce-scatter.7.cloned.1.call-done = f32[336,1024]{1,0:T(8,128)} async-done(((f32[5376,1024]{1,0:T(8,128)}), f32[336,1024]{1,0:T(8,128)}) %reduce-scatter.7.cloned.1.call-update) | async-done | bytes 1376272
  516.6 1.8 copy.59
  518.6 1.5 copy.42
  (52 shorter events, 5.3 us)
Async XLA Ops:
  7.2 94.5 %copy-start = (bf16[128,8,128]{2,1,0:T(8,128)(2,1)S(1)}, bf16[128,8,128]{2,1,0:T(8,128)(2,1)}, u32[]{:S(2)}) copy-start(bf16[128,8,128]{2,1,0:T(8,128)(2,1)} %param.6) | copy-start | bytes 786436
  7.2 19.1 %copy-start.8 = (s32[2048]{0:T(1024)S(1)}, s32[2048]{0:T(1024)}, u32[]{:S(2)}) copy-start(s32[2048]{0:T(1024)} %param.11) | copy-start | bytes 24580
  7.2 102.8 %all-gather.5.cloned.1.call-start = ((), (), s32[]{:S(2)}) async-start(), calls=%async_computation.4 | async-start | bytes 2064384 | tf_op jit(solution)/shard_map/all_gather | solution.py:64
  7.9 135.9 %all-gather.3.cloned.1.call-start = ((), (), s32[]{:S(2)}) async-start(), calls=%async_computation.2 | async-start | bytes 11698176 | tf_op jit(solution)/shard_map/all_gather | solution.py:57
  8.7 407.9 %reduce-scatter.5.cloned.1.call-start = ((), (), s32[]{:S(2)}) async-start(), calls=%async_computation.3 | async-start | bytes 4128768 | tf_op jit(solution)/shard_map/reduce_scatter | solution.py:61
  9.8 90.4 %collective-permute-start.7 = (bf16[2,128,4,128]{3,1,2,0:T(8,128)(2,1)S(1)}, bf16[2,128,4,128]{3,1,2,0:T(8,128)(2,1)S(1)}, u32[]{:S(2)}, u32[]{:S(2)}) collective-permute-start(bf16[2,128,4,128]{3,1,2,0:T(8,128)(2,1)S(1)} %pad_maximum_fusion.1), channel_id=1, source_target_pairs={{0,2},{2,4},{4,6},{6,8},{8,10},{10,12},{12,14},{14,16},{16,18},{18... | collective-permute-start | bytes 786440 | tf_op jit(solution)/shard_map/ppermute | solution.py:12
  12.1 87.9 %collective-permute-start.6 = (bf16[2,128,4,128]{3,1,2,0:T(8,128)(2,1)S(1)}, bf16[2,128,4,128]{3,1,2,0:T(8,128)(2,1)S(1)}, u32[]{:S(2)}, u32[]{:S(2)}) collective-permute-start(bf16[2,128,4,128]{3,1,2,0:T(8,128)(2,1)S(1)} %pad_maximum_fusion.1), channel_id=1, source_target_pairs={{0,4},{2,6},{4,8},{6,10},{8,12},{10,14},{12,16},{14,18},{16,20},{1... | collective-permute-start | bytes 786440 | tf_op jit(solution)/shard_map/ppermute | solution.py:12
  16.6 35.4 %collective-permute-start.2 = (bf16[2,128,4,128]{3,1,2,0:T(8,128)(2,1)S(1)}, bf16[2,128,4,128]{3,1,2,0:T(8,128)(2,1)S(1)}, u32[]{:S(2)}, u32[]{:S(2)}) collective-permute-start(bf16[2,128,4,128]{3,1,2,0:T(8,128)(2,1)S(1)} %pad_maximum_fusion.1), channel_id=1, source_target_pairs={{0,12},{2,14},{4,16},{6,18},{8,20},{10,22},{12,24},{14,26},{16,28}... | collective-permute-start | bytes 786440 | tf_op jit(solution)/shard_map/ppermute | solution.py:12
  21.0 29.6 %collective-permute-start.1 = (bf16[2,128,4,128]{3,1,2,0:T(8,128)(2,1)S(1)}, bf16[2,128,4,128]{3,1,2,0:T(8,128)(2,1)S(1)}, u32[]{:S(2)}, u32[]{:S(2)}) collective-permute-start(bf16[2,128,4,128]{3,1,2,0:T(8,128)(2,1)S(1)} %pad_maximum_fusion.1), channel_id=1, source_target_pairs={{0,14},{2,16},{4,18},{6,20},{8,22},{10,24},{12,26},{14,28},{16,30}... | collective-permute-start | bytes 786440 | tf_op jit(solution)/shard_map/ppermute | solution.py:12
  24.9 13.8 %collective-permute-start = (bf16[2,128,4,128]{3,1,2,0:T(8,128)(2,1)S(1)}, bf16[2,128,4,128]{3,1,2,0:T(8,128)(2,1)S(1)}, u32[]{:S(2)}, u32[]{:S(2)}) collective-permute-start(bf16[2,128,4,128]{3,1,2,0:T(8,128)(2,1)S(1)} %pad_maximum_fusion.1), channel_id=1, source_target_pairs={{0,16},{2,18},{4,20},{6,22},{8,24},{10,26},{12,28},{14,30},{1,17},... | collective-permute-start | bytes 786440 | tf_op jit(solution)/shard_map/ppermute | solution.py:12
  38.7 51.9 %collective-permute-start.3 = (bf16[2,128,4,128]{3,1,2,0:T(8,128)(2,1)S(1)}, bf16[2,128,4,128]{3,1,2,0:T(8,128)(2,1)S(1)}, u32[]{:S(2)}, u32[]{:S(2)}) collective-permute-start(bf16[2,128,4,128]{3,1,2,0:T(8,128)(2,1)S(1)} %pad_maximum_fusion.1), channel_id=1, source_target_pairs={{0,10},{2,12},{4,14},{6,16},{8,18},{10,20},{12,22},{14,24},{16,26}... | collective-permute-start | bytes 786440 | tf_op jit(solution)/shard_map/ppermute | solution.py:12
  50.7 40.0 %collective-permute-start.4 = (bf16[2,128,4,128]{3,1,2,0:T(8,128)(2,1)S(1)}, bf16[2,128,4,128]{3,1,2,0:T(8,128)(2,1)S(1)}, u32[]{:S(2)}, u32[]{:S(2)}) collective-permute-start(bf16[2,128,4,128]{3,1,2,0:T(8,128)(2,1)S(1)} %pad_maximum_fusion.1), channel_id=1, source_target_pairs={{0,8},{2,10},{4,12},{6,14},{8,16},{10,18},{12,20},{14,22},{16,24},... | collective-permute-start | bytes 786440 | tf_op jit(solution)/shard_map/ppermute | solution.py:12
  52.0 48.0 %collective-permute-start.5 = (bf16[2,128,4,128]{3,1,2,0:T(8,128)(2,1)S(1)}, bf16[2,128,4,128]{3,1,2,0:T(8,128)(2,1)S(1)}, u32[]{:S(2)}, u32[]{:S(2)}) collective-permute-start(bf16[2,128,4,128]{3,1,2,0:T(8,128)(2,1)S(1)} %pad_maximum_fusion.1), channel_id=1, source_target_pairs={{0,6},{2,8},{4,10},{6,12},{8,14},{10,16},{12,18},{14,20},{16,22},{... | collective-permute-start | bytes 786440 | tf_op jit(solution)/shard_map/ppermute | solution.py:12
  100.2 1.4 copy-start.5
  109.9 40.2 %copy-start.3 = (bf16[4,2,128,1152]{2,3,1,0:T(8,128)(2,1)}, bf16[4,2,128,1152]{2,3,1,0:T(8,128)(2,1)S(1)}, u32[]{:S(2)}) copy-start(bf16[4,2,128,1152]{2,3,1,0:T(8,128)(2,1)S(1)} %fusion.9) | copy-start | bytes 7077892
  161.5 1.3 copy-start.2
  161.5 355.1 %reduce-scatter.7.cloned.1.call-start = ((), (), s32[]{:S(2)}) async-start(), calls=%async_computation.5 | async-start | bytes 23396352
  193.7 1.7 copy-start.6
  198.5 1.7 copy-start.4
  200.9 2.5 copy-start.1
  200.9 32.8 %copy-start.7 = (bf16[2,1152,4,128]{3,1,2,0:T(8,128)(2,1)S(1)}, bf16[2,1152,4,128]{3,1,2,0:T(8,128)(2,1)}, u32[]{:S(2)}) copy-start(bf16[2,1152,4,128]{3,1,2,0:T(8,128)(2,1)} %copy-done.5) | copy-start | bytes 7077892
  203.4 6.5 %collective-permute-start.8 = (f32[2,128,4,128]{3,1,2,0:T(8,128)S(1)}, f32[2,128,4,128]{3,1,2,0:T(8,128)S(1)}, u32[]{:S(2)}, u32[]{:S(2)}) collective-permute-start(f32[2,128,4,128]{3,1,2,0:T(8,128)S(1)} %get-tuple-element.15), channel_id=1, source_target_pairs={{2,0},{4,2},{6,4},{8,6},{10,8},{12,10},{14,12},{16,14},{18,16},{20... | collective-permute-start | bytes 1572872 | tf_op jit(solution)/shard_map/ppermute | solution.py:12
  204.7 25.9 %collective-permute-start.9 = (f32[2,128,4,128]{3,1,2,0:T(8,128)S(1)}, f32[2,128,4,128]{3,1,2,0:T(8,128)}, u32[]{:S(2)}, u32[]{:S(2)}) collective-permute-start(f32[2,128,4,128]{3,1,2,0:T(8,128)S(1)} %get-tuple-element.16), channel_id=1, source_target_pairs={{4,0},{6,2},{8,4},{10,6},{12,8},{14,10},{16,12},{18,14},{20,16},{2... | collective-permute-start | bytes 1572872 | tf_op jit(solution)/shard_map/ppermute | solution.py:12
  206.0 26.4 %collective-permute-start.10 = (f32[2,128,4,128]{3,1,2,0:T(8,128)S(1)}, f32[2,128,4,128]{3,1,2,0:T(8,128)}, u32[]{:S(2)}, u32[]{:S(2)}) collective-permute-start(f32[2,128,4,128]{3,1,2,0:T(8,128)S(1)} %get-tuple-element.17), channel_id=1, source_target_pairs={{6,0},{8,2},{10,4},{12,6},{14,8},{16,10},{18,12},{20,14},{22,16},{... | collective-permute-start | bytes 1572872 | tf_op jit(solution)/shard_map/ppermute | solution.py:12
  207.3 46.8 %collective-permute-start.11 = (f32[2,128,4,128]{3,1,2,0:T(8,128)}, f32[2,128,4,128]{3,1,2,0:T(8,128)}, u32[]{:S(2)}, u32[]{:S(2)}) collective-permute-start(f32[2,128,4,128]{3,1,2,0:T(8,128)} %get-tuple-element.18), channel_id=1, source_target_pairs={{8,0},{10,2},{12,4},{14,6},{16,8},{18,10},{20,12},{22,14},{24,16},... | collective-permute-start | bytes 1572872 | tf_op jit(solution)/shard_map/ppermute | solution.py:12
  208.6 50.3 %collective-permute-start.12 = (f32[2,128,4,128]{3,1,2,0:T(8,128)}, f32[2,128,4,128]{3,1,2,0:T(8,128)}, u32[]{:S(2)}, u32[]{:S(2)}) collective-permute-start(f32[2,128,4,128]{3,1,2,0:T(8,128)} %get-tuple-element.19), channel_id=1, source_target_pairs={{10,0},{12,2},{14,4},{16,6},{18,8},{20,10},{22,12},{24,14},{26,16}... | collective-permute-start | bytes 1572872 | tf_op jit(solution)/shard_map/ppermute | solution.py:12
  209.9 61.9 %collective-permute-start.13 = (f32[2,128,4,128]{3,1,2,0:T(8,128)}, f32[2,128,4,128]{3,1,2,0:T(8,128)}, u32[]{:S(2)}, u32[]{:S(2)}) collective-permute-start(f32[2,128,4,128]{3,1,2,0:T(8,128)} %get-tuple-element.20), channel_id=1, source_target_pairs={{12,0},{14,2},{16,4},{18,6},{20,8},{22,10},{24,12},{26,14},{28,16}... | collective-permute-start | bytes 1572872 | tf_op jit(solution)/shard_map/ppermute | solution.py:12
  230.6 182.0 %collective-permute-start.15 = (f32[2,128,4,128]{3,1,2,0:T(8,128)}, f32[2,128,4,128]{3,1,2,0:T(8,128)}, u32[]{:S(2)}, u32[]{:S(2)}) collective-permute-start(f32[2,128,4,128]{3,1,2,0:T(8,128)} %get-tuple-element.21), channel_id=1, source_target_pairs={{16,0},{18,2},{20,4},{22,6},{24,8},{26,10},{28,12},{30,14},{17,1},... | collective-permute-start | bytes 1572872 | tf_op jit(solution)/shard_map/ppermute | solution.py:12
  232.4 180.2 %collective-permute-start.14 = (f32[2,128,4,128]{3,1,2,0:T(8,128)}, f32[2,128,4,128]{3,1,2,0:T(8,128)}, u32[]{:S(2)}, u32[]{:S(2)}) collective-permute-start(f32[2,128,4,128]{3,1,2,0:T(8,128)} %get-tuple-element.22), channel_id=1, source_target_pairs={{14,0},{16,2},{18,4},{20,6},{22,8},{24,10},{26,12},{28,14},{30,16}... | collective-permute-start | bytes 1572872 | tf_op jit(solution)/shard_map/ppermute | solution.py:12
Sparse Core Ops, SparseCore 0:
  9.6 27.6 all-gather.4
  39.6 104.1 all-gather.2
  161.6 46.4 reduce-scatter.4
  212.8 303.7 reduce-scatter.6
where the time goes:
time: 528 us; the launch traced here: 527 us
  waiting for transfers between devices  351 us (66%)
  starting transfers between devices  78.8 us (15%)
  matrix products  37.2 us (7%)
  local copies, waits for them, and re-layouts  35.1 us (7%)
  between operations  14.2 us (3%)
  other arithmetic  10.4 us (2%)
    ppermute x16, waiting for transfers between devices, passed_along(): return lax.ppermute(value, axis, pairs)  218 us
    unnamed x5, waiting for transfers between devices  99.2 us
    ppermute x16, starting transfers between devices, passed_along(): return lax.ppermute(value, axis, pairs)  78.5 us
    unnamed x32, local copies, waits for them, and re-layouts  33.9 us
    all_gather x1, waiting for transfers between devices, shards(): proj_full = lax.all_gather(out_proj, 'ctx', axis=0, tiled=True)  33.8 us
  transfers between devices with their start and end apart: 20, of which 10 were waited for; matrix products, arithmetic and copies ran while one was open for 11% of the time, Pallas kernels for 0%

commit v1 on v0

v1 whole, which is shorter than its diff:
```python
import jax
import jax.numpy as jnp
from jax import lax
from jax.sharding import PartitionSpec as P

WINDOW_TOKENS = 1024
BF16 = jnp.bfloat16
F32 = jnp.float32


def shifted(value, axis, by):
    count = lax.axis_size(axis)
    pairs = [(i, i + by) for i in range(count) if 0 <= i + by < count]
    return lax.ppermute(value, axis, pairs)


def rotated(value, axis, by):
    count = lax.axis_size(axis)
    return lax.ppermute(value, axis, [(i, (i + by) % count) for i in range(count)])


def matmul(a, b, dims):
    return lax.dot_general(a, b, (dims, ((), ())), preferred_element_type=F32)


def shards(queries, rotated_keys, value_vectors, out_grad, out_proj, seg_ids):
    logit_scale = 168.0 ** (-0.5)
    tok_rows, heads_query, head_size = queries.shape
    heads_kv = rotated_keys.shape[1]
    per_kv = heads_query // heads_kv
    ctx_count = lax.axis_size("ctx")
    head_count = lax.axis_size("head")
    ctx_index = lax.axis_index("ctx")
    head_index = lax.axis_index("head")
    group = heads_kv
    groups = [[g * group + i for i in range(group)] for g in range(ctx_count // group)]
    rows = group * tok_rows
    halo_blocks = WINDOW_TOKENS // rows
    q_width = per_kv * head_size

    def to_heads(value):
        return lax.all_to_all(value, "ctx", 1, 0, axis_index_groups=groups, tiled=True)

    def to_tokens(value):
        return lax.all_to_all(value, "ctx", 0, 1, axis_index_groups=groups, tiled=True)

    packed = jnp.concatenate(
        [queries.reshape(tok_rows, heads_kv, q_width), rotated_keys, value_vectors], axis=2
    )
    mine = to_heads(packed).reshape(rows, q_width + 2 * head_size)
    q = mine[:, :q_width].reshape(rows, per_kv, head_size).transpose(1, 0, 2)
    own_kv = mine[:, q_width:]
    received = [shifted(own_kv, "ctx", group * (d + 1)) for d in range(halo_blocks)]
    kv = jnp.concatenate(received[::-1] + [own_kv], axis=0)
    keys, values = kv[:, :head_size], kv[:, head_size:]

    proj_full = lax.all_gather(out_proj, "ctx", axis=0, tiled=True)

    columns = out_grad.shape[1]
    grad_full = jnp.zeros((tok_rows, columns * head_count), BF16)
    grad_full = lax.dynamic_update_slice_in_dim(grad_full, out_grad, head_index * columns, 1)
    for d in range(1, head_count):
        block = rotated(out_grad, "head", d)
        source = lax.rem(head_index + head_count - d, head_count)
        grad_full = lax.dynamic_update_slice_in_dim(grad_full, block, source * columns, 1)
    grad_columns = lax.all_to_all(grad_full, "ctx", 1, 0, tiled=True)

    first_row = (ctx_index // group) * rows
    seg_padded = jnp.concatenate([jnp.full((WINDOW_TOKENS,), -1, jnp.int32), seg_ids], 0)
    key_seg = lax.dynamic_slice_in_dim(seg_padded, first_row, WINDOW_TOKENS + rows, 0)
    query_seg = lax.dynamic_slice_in_dim(seg_ids, first_row, rows, 0)
    query_pos = first_row + jnp.arange(rows, dtype=jnp.int32)
    key_pos = first_row - WINDOW_TOKENS + jnp.arange(WINDOW_TOKENS + rows, dtype=jnp.int32)
    allowed = (key_pos[None, :] <= query_pos[:, None]) & (
        query_pos[:, None] - key_pos[None, :] < WINDOW_TOKENS
    )
    allowed = allowed & (key_pos[None, :] >= 0) & (query_seg[:, None] == key_seg[None, :])

    scores = logit_scale * jnp.einsum("htd,sd->hts", q, keys, preferred_element_type=F32)
    scores = jnp.where(allowed, scores, -1e30)
    top_score = jnp.max(scores, axis=2, keepdims=True)
    weights = jnp.where(allowed, jnp.exp(scores - top_score), 0.0)
    probs = weights / jnp.sum(weights, axis=2, keepdims=True)
    probs_bf = probs.astype(BF16)
    attended = jnp.einsum("hts,sd->htd", probs_bf, values, preferred_element_type=F32).astype(BF16)
    attended_tok = to_tokens(attended.transpose(1, 0, 2).reshape(rows, q_width))
    attended_all = lax.all_gather(attended_tok, "ctx", axis=0, tiled=True)

    grad_att_tok = matmul(grad_full, proj_full, ((1,), (0,))).astype(BF16)
    grad_att = to_heads(grad_att_tok).reshape(rows, per_kv, head_size).transpose(1, 0, 2)

    def out_columns(which):
        block = lax.dynamic_slice_in_dim(proj_full, which * columns, columns, 0)
        return matmul(attended_tok, block, ((1,), (1,)))

    layer_out = out_columns(head_index)
    for d in range(1, head_count):
        target = lax.rem(head_index + d, head_count)
        layer_out = layer_out + rotated(out_columns(target).astype(BF16), "head", d).astype(F32)
    layer_out = layer_out.astype(BF16)

    grad_proj = matmul(grad_columns, attended_all, ((0,), (0,))) * (ctx_count * tok_rows) ** (-0.5)

    grad_probs = jnp.einsum("htd,sd->hts", grad_att, values, preferred_element_type=F32)
    row_delta = jnp.sum(grad_att.astype(F32) * attended.astype(F32), axis=2, keepdims=True)
    grad_scores = (probs * (grad_probs - row_delta)).astype(BF16)
    grad_k = logit_scale * jnp.einsum("hts,htd->sd", grad_scores, q, preferred_element_type=F32)
    grad_v = jnp.einsum("hts,htd->sd", probs_bf, grad_att, preferred_element_type=F32)
    grad_kv = jnp.concatenate([grad_k, grad_v], axis=1)
    own_grad = grad_kv[WINDOW_TOKENS:]
    for d in range(1, halo_blocks + 1):
        start = WINDOW_TOKENS - d * rows
        own_grad = own_grad + shifted(
            grad_kv[start : start + rows].astype(BF16), "ctx", -group * d
        ).astype(F32)
    grad_q = logit_scale * jnp.einsum("hts,sd->thd", grad_scores, keys, preferred_element_type=F32)
    grads = jnp.concatenate([grad_q.astype(BF16).reshape(rows, q_width), own_grad.astype(BF16)], 1)
    grads = to_tokens(grads).reshape(tok_rows, heads_kv, q_width + 2 * head_size)
    query_gradient = grads[:, :, :q_width].reshape(tok_rows, heads_query, head_size)
    grad_key = grads[:, :, q_width : q_width + head_size]
    grad_value = grads[:, :, q_width + head_size :]
    return (layer_out, query_gradient, grad_key, grad_value, grad_proj)


def solution(mesh):
    tokens_heads = P("ctx", "head", None)
    both = P("ctx", "head")
    return jax.shard_map(
        shards,
        mesh=mesh,
        in_specs=(tokens_heads, tokens_heads, tokens_heads, both, both, P()),
        out_specs=(both, tokens_heads, tokens_heads, tokens_heads, both),
        check_vma=False,
    )
```

time: 528 us -> 250 us (0.47)
  waiting for transfers between devices: 351 us -> 120 us
  starting transfers between devices: 78.8 us -> 27.2 us
  blocking collectives: 0 us -> 26.3 us
  local copies, waits for them, and re-layouts: 35.1 us -> 15.8 us
    ppermute x16 -> x6, waiting for transfers between devices: 218 us -> 54.6 us  [the longest x4 41 us: shifted(): return lax.ppermute(value, axis, pairs)]
    unnamed x5 -> x2, waiting for transfers between devices: 99.2 us -> 0.7 us
    ppermute x16 -> x6, starting transfers between devices: 78.5 us -> 15.8 us  [the longest x4 12.1 us: shifted(): return lax.ppermute(value, axis, pairs)]
    unnamed x32 -> x25, local copies, waits for them, and re-layouts: 33.9 us -> 5.28 us
    all_to_all x0 -> x2, blocking collectives: none -> 26.3 us  [to_tokens(): lax.all_to_all(value, 'ctx', 0, 1, axis_index_groups=groups, tiled=True)]
    all_gather x1, waiting for transfers between devices: 33.8 us -> 56.4 us  [shards(): proj_full = lax.all_gather(out_proj, 'ctx', axis=0, tiled=True)]
    all_to_all x0 -> x3, starting transfers between devices: none -> 11.3 us  [the longest x2 7.64 us: to_heads(): lax.all_to_all(value, 'ctx', 1, 0, axis_index_groups=groups, tiled=True)]
    all_to_all x0 -> x3, waiting for transfers between devices: none -> 8.74 us  [the longest x2 8.73 us: to_heads(): lax.all_to_all(value, 'ctx', 1, 0, axis_index_groups=groups, tiled=True)]
  transfers between devices with their start and end apart: 20 -> 11, of which waited for: 10 -> 8; matrix products, arithmetic and copies ran while one was open for 11% -> 15% of each run, Pallas kernels for 0% -> 0%
where the time goes in v1:
time: 250 us; the launch traced here: 246 us
  waiting for transfers between devices  120 us (48%)
  matrix products  36.3 us (15%)
  starting transfers between devices  27.2 us (11%)
  blocking collectives  26.3 us (11%)
  local copies, waits for them, and re-layouts  15.8 us (6%)
  between operations  14.3 us (6%)
  other arithmetic  6 us (2%)
    all_gather x1, waiting for transfers between devices, shards(): proj_full = lax.all_gather(out_proj, 'ctx', axis=0, tiled=True)  56.4 us
    ppermute x4, waiting for transfers between devices, shifted(): return lax.ppermute(value, axis, pairs)  41 us
    all_to_all x2, blocking collectives, to_tokens(): lax.all_to_all(value, 'ctx', 0, 1, axis_index_groups=groups, tiled=True)  26.3 us
    dot_general x4, matrix products, matmul(): return lax.dot_general(a, b, (dims, ((), ())), preferred_element_type=F32)  21.7 us
    ppermute x2, waiting for transfers between devices, rotated(): lax.ppermute(value, axis, [(i, (i + by) % count) for i in range(count)])  13.6 us
    ppermute x4, starting transfers between devices, shifted(): return lax.ppermute(value, axis, pairs)  12.1 us
    all_to_all x2, waiting for transfers between devices, to_heads(): lax.all_to_all(value, 'ctx', 1, 0, axis_index_groups=groups, tiled=True)  8.73 us
    all_to_all x2, starting transfers between devices, to_heads(): lax.all_to_all(value, 'ctx', 1, 0, axis_index_groups=groups, tiled=True)  7.64 us
  transfers between devices with their start and end apart: 11, of which 8 were waited for; matrix products, arithmetic and copies ran while one was open for 15% of the time, Pallas kernels for 0%

profile of v1, /device:TPU:0, one launch (start us, length us, event | category | flops | bytes accessed | tf_op | source)
XLA Modules:
  0.0 246.3 jit_solution(17306477290051257502)
XLA Ops:
  7.2 0.7 all-gather.3.cloned.1.call-update
  7.9 0.9 copy.56
  8.8 0.9 copy.57
  9.8 1.1 reshape.64
  10.9 0.8 pad_maximum_fusion.2
  11.8 4.2 %all-to-all-start = ((bf16[128,4,512]{2,0,1:T(8,128)(2,1)}), bf16[128,4,512]{2,0,1:T(8,128)(2,1)S(1)}, u32[]{:S(2)}, u32[]{:S(2)}) async-start(bf16[128,4,512]{2,0,1:T(8,128)(2,1)} %pad_maximum_fusion.2), calls=%async_computation | async-start | bytes 1048576 | tf_op jit(solution)/shard_map/all_to_all | solution.py:42
  16.4 2.2 collective-permute-start.3
  18.8 1.2 fusion.13
  20.0 6.4 %all-to-all-done = bf16[128,4,512]{2,0,1:T(8,128)(2,1)S(1)} async-done(((bf16[128,4,512]{2,0,1:T(8,128)(2,1)}), bf16[128,4,512]{2,0,1:T(8,128)(2,1)S(1)}, u32[]{:S(2)}, u32[]{:S(2)}) %all-to-all-start) | async-done | bytes 524320 | tf_op jit(solution)/shard_map/all_to_all | solution.py:42
  26.4 4.7 %collective-permute-start.1 = (bf16[512,256]{1,0:T(8,128)(2,1)S(1)}, bf16[512,256]{1,0:T(8,128)(2,1)S(1)}, u32[]{:S(2)}, u32[]{:S(2)}) collective-permute-start(bf16[512,256]{1,0:T(8,128)(2,1)S(1)} %get-tuple-element.20), channel_id=1, source_target_pairs={{0,8},{2,10},{4,12},{6,14},{8,16},{10,18},{12,20},{14,22},{16,24},... | collective-permute-start | bytes 786440 | tf_op jit(solution)/shard_map/ppermute | solution.py:14
  31.1 4.7 %collective-permute-start = (bf16[512,256]{1,0:T(8,128)(2,1)S(1)}, bf16[512,256]{1,0:T(8,128)(2,1)S(1)}, u32[]{:S(2)}, u32[]{:S(2)}) collective-permute-start(bf16[512,256]{1,0:T(8,128)(2,1)S(1)} %get-tuple-element.20), channel_id=1, source_target_pairs={{0,16},{2,18},{4,20},{6,22},{8,24},{10,26},{12,28},{14,30},{1,17},... | collective-permute-start | bytes 786440 | tf_op jit(solution)/shard_map/ppermute | solution.py:14
  35.8 1.3 broadcast_in_dim.29
  37.1 0.9 constant_dynamic-update-slice_fusion.1
  38.0 5.4 %collective-permute-done.1 = bf16[512,256]{1,0:T(8,128)(2,1)S(1)} collective-permute-done((bf16[512,256]{1,0:T(8,128)(2,1)S(1)}, bf16[512,256]{1,0:T(8,128)(2,1)S(1)}, u32[]{:S(2)}, u32[]{:S(2)}) %collective-permute-start.1) | collective-permute-done | bytes 262176 | tf_op jit(solution)/shard_map/ppermute | solution.py:14
  43.4 10.5 %collective-permute-done = bf16[512,256]{1,0:T(8,128)(2,1)S(1)} collective-permute-done((bf16[512,256]{1,0:T(8,128)(2,1)S(1)}, bf16[512,256]{1,0:T(8,128)(2,1)S(1)}, u32[]{:S(2)}, u32[]{:S(2)}) %collective-permute-start) | collective-permute-done | bytes 262176 | tf_op jit(solution)/shard_map/ppermute | solution.py:14
  54.0 5.7 %fusion.43 = (f32[2,512]{1,0:T(2,128)S(1)}, f32[2,512,1536]{2,1,0:T(8,128)}) fusion(pred[512,1536]{1,0:T(8,128)(4,1)S(1)} %fusion.13, bf16[1536,256]{1,0:T(8,128)(2,1)S(1)} %pad_maximum_fusion.1, bf16[64,2,8,128]{3,2,1,0:T(8,128)(2,1)S(1)} %get-tuple-element.19), kind=kOutput, calls=%fused_computation.66 | convolution fusion | flops 410519040 | bytes 8523776 | tf_op jit(solution)/shard_map/sub | solution.py:82
  59.7 0.9 constant_dynamic-update-slice_fusion
  60.6 56.4 %all-gather.3.cloned.1.call-done = bf16[5376,1024]{1,0:T(8,128)(2,1)} async-done(((bf16[336,1024]{1,0:T(8,128)(2,1)}), bf16[5376,1024]{1,0:T(8,128)(2,1)}) %all-gather.3.cloned.1.call-update) | async-done | bytes 11010064 | tf_op jit(solution)/shard_map/all_gather | solution.py:57
  117.0 6.2 %convolution_convert_fusion.1 = bf16[128,1024]{1,0:T(8,128)(2,1)S(1)} fusion(bf16[128,5376]{0,1:T(8,128)(2,1)} %constant_dynamic-update-slice_fusion, bf16[5376,1024]{1,0:T(8,128)(2,1)} %all-gather.3.cloned.1.call-done), kind=kOutput, calls=%fused_computation.33 | convolution fusion | flops 1409417216 | bytes 12648448 | tf_op jit(solution)/shard_map/dot_general | solution.py:23
  123.2 0.8 copy.81
  124.0 3.4 %all-to-all-start.2 = ((bf16[128,4,256]{0,2,1:T(8,128)(2,1)}), bf16[128,4,256]{0,2,1:T(8,128)(2,1)S(1)}, u32[]{:S(2)}, u32[]{:S(2)}) async-start(bf16[128,4,256]{0,2,1:T(8,128)(2,1)} %bitcast.13), calls=%async_computation.2 | async-start | bytes 524288 | tf_op jit(solution)/shard_map/all_to_all | solution.py:42
  127.5 3.6 %fusion.15 = bf16[2,512,1536]{2,1,0:T(8,128)(2,1)S(1)} fusion(f32[2,512,1536]{2,1,0:T(8,128)} %get-tuple-element.22, f32[2,512]{1,0:T(2,128)S(1)} %get-tuple-element.21), kind=kLoop, calls=%fused_computation.18 | loop fusion | flops 3145728 | bytes 9441280 | tf_op jit(solution)/shard_map/convert_element_type | solution.py:84
  131.1 2.4 all-to-all-done.2
  133.4 0.9 copy.64
  134.3 1.1 reshape.67
  135.4 2.9 %multiply_reduce_fusion = (f32[2,512]{1,0:T(2,128)S(1)}, bf16[2,512,128]{1,2,0:T(8,128)(2,1)}) fusion(bf16[512,2,128]{0,2,1:T(8,128)(2,1)S(1)} %reshape.67, bf16[2,512,1536]{2,1,0:T(8,128)(2,1)S(1)} %fusion.15, bf16[1536,256]{1,0:T(8,128)(2,1)} %copy-done.3), kind=kOutput, calls=%fused_computation.43 | convolution fusion | flops 403307520 | bytes 4067328 | tf_op jit(solution)/shard_map/hts,sd->htd/dot_general | solution.py:85
  138.2 1.7 all_to_all.64
  140.0 1.0 copy.60
  141.0 9.1 %all_to_all.82 = bf16[4,128,256]{1,2,0:T(8,128)(2,1)} all-to-all(bf16[4,128,256]{1,2,0:T(8,128)(2,1)S(1)} %copy.60), channel_id=1, replica_groups={{0,2,4,6},{8,10,12,14},{16,18,20,22},{24,26,28,30},{1,3,5,7},{9,11,13,1..., dimensions={0} | all-to-all | bytes 524288 | tf_op jit(solution)/shard_map/all_to_all | solution.py:45
  150.1 0.6 convolution_bitcast_fusion
  150.7 0.5 copy-done.4
  151.2 3.6 %multiply_convert_fusion = bf16[2,512,1536]{2,1,0:T(8,128)(2,1)S(1)} fusion(f32[2,512]{1,0:T(2,128)S(1)} %get-tuple-element.23, f32[2,512,1536]{2,1,0:T(8,128)} %get-tuple-element.22, f32[2,512]{1,0:T(2,128)S(1)} %get-tuple-element.21, bf16[1536,256]{1,0:T(8,128)(2,1)S(1)} %copy-done.4, bf16[512,2,128]{0,2,1:T(8,128)(2,1)S(1)} %reshape.67), kind=kOutput, calls=%fused_computation.1 | convolution fusion | flops 408944640 | bytes 10100736 | tf_op jit(solution)/shard_map/htd,sd->hts/dot_general | solution.py:104
  154.8 0.6 fusion.16
  155.6 1.4 collective-permute-start.4
  157.1 1.3 collective-permute-start.5
  158.4 1.2 fusion.21
  159.8 10.2 %collective-permute-done.4 = bf16[512,256]{0,1:T(8,128)(2,1)S(1)} collective-permute-done((bf16[512,256]{0,1:T(8,128)(2,1)S(1)}, bf16[512,256]{0,1:T(8,128)(2,1)S(1)}, u32[]{:S(2)}, u32[]{:S(2)}) %collective-permute-start.4) | collective-permute-done | bytes 262176 | tf_op jit(solution)/shard_map/ppermute | solution.py:14
  170.0 14.9 %collective-permute-done.5 = bf16[512,256]{0,1:T(8,128)(2,1)S(1)} collective-permute-done((bf16[512,256]{0,1:T(8,128)(2,1)S(1)}, bf16[512,256]{0,1:T(8,128)(2,1)S(1)}, u32[]{:S(2)}, u32[]{:S(2)}) %collective-permute-start.5) | collective-permute-done | bytes 262176 | tf_op jit(solution)/shard_map/ppermute | solution.py:14
  185.2 17.2 %all_to_all.83 = bf16[4,128,512]{2,1,0:T(8,128)(2,1)S(1)} all-to-all(bf16[4,128,512]{2,1,0:T(8,128)(2,1)S(1)} %pad_maximum_fusion.3), channel_id=1, replica_groups={{0,2,4,6},{8,10,12,14},{16,18,20,22},{24,26,28,30},{1,3,5,7},{9,11,13,1..., dimensions={0} | all-to-all | bytes 1048576 | tf_op jit(solution)/shard_map/all_to_all | solution.py:45
  202.4 3.7 %all-to-all-start.4 = ((bf16[128,16,336]{0,2,1:T(8,128)(2,1)}), bf16[128,16,336]{0,2,1:T(8,128)(2,1)S(1)}, u32[]{:S(2)}, u32[]{:S(2)}) async-start(bf16[128,16,336]{0,2,1:T(8,128)(2,1)} %bitcast.25), calls=%async_computation.4 | async-start | bytes 2752512 | tf_op jit(solution)/shard_map/all_to_all | solution.py:66
  206.1 5.3 %fusion.6 = bf16[128,2688]{1,0:T(8,128)(2,1)} fusion(bf16[128,1024]{0,1:T(8,128)(2,1)S(1)} %bitcast.93, bf16[5376,1024]{1,0:T(8,128)(2,1)} %all-gather.3.cloned.1.call-done, s32[]{:T(128)S(6)} %select_n.32), kind=kOutput, calls=%fused_computation.9 | convolution fusion | flops 704987136 | bytes 6455300 | tf_op jit(solution)/shard_map/dot_general | solution.py:23
  211.4 1.5 collective-permute-start.2
  213.2 0.8 copy.74
  214.0 0.9 copy.72
  214.8 0.8 copy.73
  215.6 13.6 %collective-permute-done.2 = bf16[128,2688]{1,0:T(8,128)(2,1)S(1)} collective-permute-done((bf16[128,2688]{1,0:T(8,128)(2,1)}, bf16[128,2688]{1,0:T(8,128)(2,1)S(1)}, u32[]{:S(2)}, u32[]{:S(2)}) %collective-permute-start.2) | collective-permute-done | bytes 688160 | tf_op jit(solution)/shard_map/ppermute | solution.py:19
  229.2 5.3 %add_convert_fusion = bf16[128,2688]{1,0:T(8,128)(2,1)} fusion(bf16[128,2688]{1,0:T(8,128)(2,1)S(1)} %collective-permute-done.2, bf16[128,1024]{0,1:T(8,128)(2,1)S(1)} %bitcast.94, bf16[5376,1024]{1,0:T(8,128)(2,1)} %all-gather.3.cloned.1.call-done, s32[]{:T(128)S(6)} %select_n.31), kind=kOutput, calls=%fused_computation.29 | convolution fusion | flops 705675264 | bytes 7143428 | tf_op jit(solution)/shard_map/dot_general | solution.py:23
  234.6 4.9 %convolution_multiply_fusion = f32[336,1024]{1,0:T(8,128)} fusion(bf16[2048,1024]{0,1:T(8,128)(2,1)} %all-gather.5.cloned.1.call-done, bf16[128,16,336]{0,2,1:T(8,128)(2,1)S(1)} %all-to-all-done.4), kind=kOutput, calls=%fused_computation.26 | convolution fusion | flops 1409630208 | bytes 6946816 | tf_op jit(solution)/shard_map/dot_general | solution.py:23
  (41 shorter events, 1.7 us)
Async XLA Ops:
  7.2 8.9 %copy-start.7 = (bf16[128,2688]{1,0:T(8,128)(2,1)S(1)}, bf16[128,2688]{1,0:T(8,128)(2,1)}, u32[]{:S(2)}) copy-start(bf16[128,2688]{1,0:T(8,128)(2,1)} %param.9) | copy-start | bytes 2064388
  7.2 11.5 %copy-start.8 = (s32[2048]{0:T(1024)S(1)}, s32[2048]{0:T(1024)}, u32[]{:S(2)}) copy-start(s32[2048]{0:T(1024)} %param.11) | copy-start | bytes 24580
  7.2 109.8 %all-gather.3.cloned.1.call-start = ((), (), s32[]{:S(2)}) async-start(), calls=%async_computation.5 | async-start | bytes 11698176 | tf_op jit(solution)/shard_map/all_gather | solution.py:57
  11.8 14.6 %all-to-all-start = ((bf16[128,4,512]{2,0,1:T(8,128)(2,1)}), bf16[128,4,512]{2,0,1:T(8,128)(2,1)S(1)}, u32[]{:S(2)}, u32[]{:S(2)}) async-start(bf16[128,4,512]{2,0,1:T(8,128)(2,1)} %pad_maximum_fusion.2), calls=%async_computation | async-start | bytes 1048576 | tf_op jit(solution)/shard_map/all_to_all | solution.py:42
  16.4 43.3 %collective-permute-start.3 = (bf16[128,2688]{0,1:T(8,128)(2,1)S(1)}, bf16[128,2688]{0,1:T(8,128)(2,1)S(1)}, u32[]{:S(2)}, u32[]{:S(2)}) collective-permute-start(bf16[128,2688]{0,1:T(8,128)(2,1)S(1)} %copy.61), channel_id=1, source_target_pairs={{0,1},{1,0},{2,3},{3,2},{4,5},{5,4},{6,7},{7,6},{8,9},{9,8},{10,11... | collective-permute-start | bytes 2064392 | tf_op jit(solution)/shard_map/ppermute | solution.py:19
  26.4 33.3 %copy-start.5 = (bf16[64,2,8,128]{3,2,1,0:T(8,128)(2,1)}, bf16[64,2,8,128]{3,2,1,0:T(8,128)(2,1)S(1)}, u32[]{:S(2)}) copy-start(bf16[64,2,8,128]{3,2,1,0:T(8,128)(2,1)S(1)} %get-tuple-element.19) | copy-start | bytes 786436
  26.4 16.9 %collective-permute-start.1 = (bf16[512,256]{1,0:T(8,128)(2,1)S(1)}, bf16[512,256]{1,0:T(8,128)(2,1)S(1)}, u32[]{:S(2)}, u32[]{:S(2)}) collective-permute-start(bf16[512,256]{1,0:T(8,128)(2,1)S(1)} %get-tuple-element.20), channel_id=1, source_target_pairs={{0,8},{2,10},{4,12},{6,14},{8,16},{10,18},{12,20},{14,22},{16,24},... | collective-permute-start | bytes 786440 | tf_op jit(solution)/shard_map/ppermute | solution.py:14
  31.1 22.7 %collective-permute-start = (bf16[512,256]{1,0:T(8,128)(2,1)S(1)}, bf16[512,256]{1,0:T(8,128)(2,1)S(1)}, u32[]{:S(2)}, u32[]{:S(2)}) collective-permute-start(bf16[512,256]{1,0:T(8,128)(2,1)S(1)} %get-tuple-element.20), channel_id=1, source_target_pairs={{0,16},{2,18},{4,20},{6,22},{8,24},{10,26},{12,28},{14,30},{1,17},... | collective-permute-start | bytes 786440 | tf_op jit(solution)/shard_map/ppermute | solution.py:14
  54.0 5.8 %copy-start.3 = (bf16[1536,256]{1,0:T(8,128)(2,1)}, bf16[1536,256]{1,0:T(8,128)(2,1)S(1)}, u32[]{:S(2)}) copy-start(bf16[1536,256]{1,0:T(8,128)(2,1)S(1)} %pad_maximum_fusion.1) | copy-start | bytes 2359300
  124.0 9.4 %all-to-all-start.2 = ((bf16[128,4,256]{0,2,1:T(8,128)(2,1)}), bf16[128,4,256]{0,2,1:T(8,128)(2,1)S(1)}, u32[]{:S(2)}, u32[]{:S(2)}) async-start(bf16[128,4,256]{0,2,1:T(8,128)(2,1)} %bitcast.13), calls=%async_computation.2 | async-start | bytes 524288 | tf_op jit(solution)/shard_map/all_to_all | solution.py:42
  127.4 107.1 %all-gather.5.cloned.1.call-start = ((), (), s32[]{:S(2)}) async-start(), calls=%async_computation.6 | async-start | bytes 4456448 | tf_op jit(solution)/shard_map/all_gather | solution.py:87
  150.1 1.1 copy-start.4
  150.7 4.8 %copy-start = (f32[1536,128]{0,1:T(8,128)}, f32[1536,128]{0,1:T(8,128)S(1)}, u32[]{:S(2)}) copy-start(f32[1536,128]{0,1:T(8,128)S(1)} %convolution_bitcast_fusion) | copy-start | bytes 2359300
  151.2 3.6 %copy-start.6 = (bf16[64,2,8,128]{3,2,1,0:T(8,128)(2,1)S(1)}, bf16[64,2,8,128]{3,2,1,0:T(8,128)(2,1)}, u32[]{:S(2)}) copy-start(bf16[64,2,8,128]{3,2,1,0:T(8,128)(2,1)} %copy-done.5) | copy-start | bytes 786436
  155.6 29.3 %copy-start.1 = (f32[1536,128]{0,1:T(8,128)S(1)}, f32[1536,128]{0,1:T(8,128)}, u32[]{:S(2)}) copy-start(f32[1536,128]{0,1:T(8,128)} %copy-done) | copy-start | bytes 2359300
  155.6 14.4 %collective-permute-start.4 = (bf16[512,256]{0,1:T(8,128)(2,1)S(1)}, bf16[512,256]{0,1:T(8,128)(2,1)S(1)}, u32[]{:S(2)}, u32[]{:S(2)}) collective-permute-start(bf16[512,256]{0,1:T(8,128)(2,1)S(1)} %get-tuple-element.15), channel_id=1, source_target_pairs={{8,0},{10,2},{12,4},{14,6},{16,8},{18,10},{20,12},{22,14},{24,16},... | collective-permute-start | bytes 786440 | tf_op jit(solution)/shard_map/ppermute | solution.py:14
  157.1 27.8 %collective-permute-start.5 = (bf16[512,256]{0,1:T(8,128)(2,1)S(1)}, bf16[512,256]{0,1:T(8,128)(2,1)S(1)}, u32[]{:S(2)}, u32[]{:S(2)}) collective-permute-start(bf16[512,256]{0,1:T(8,128)(2,1)S(1)} %get-tuple-element.16), channel_id=1, source_target_pairs={{16,0},{18,2},{20,4},{22,6},{24,8},{26,10},{28,12},{30,14},{17,1},... | collective-permute-start | bytes 786440 | tf_op jit(solution)/shard_map/ppermute | solution.py:14
  185.0 21.1 %copy-start.2 = (bf16[4,128,256]{1,2,0:T(8,128)(2,1)S(1)}, bf16[4,128,256]{1,2,0:T(8,128)(2,1)}, u32[]{:S(2)}) copy-start(bf16[4,128,256]{1,2,0:T(8,128)(2,1)} %all_to_all.82) | copy-start | bytes 786436
  202.4 32.2 %all-to-all-start.4 = ((bf16[128,16,336]{0,2,1:T(8,128)(2,1)}), bf16[128,16,336]{0,2,1:T(8,128)(2,1)S(1)}, u32[]{:S(2)}, u32[]{:S(2)}) async-start(bf16[128,16,336]{0,2,1:T(8,128)(2,1)} %bitcast.25), calls=%async_computation.4 | async-start | bytes 2752512 | tf_op jit(solution)/shard_map/all_to_all | solution.py:66
  211.4 17.9 %collective-permute-start.2 = (bf16[128,2688]{1,0:T(8,128)(2,1)}, bf16[128,2688]{1,0:T(8,128)(2,1)S(1)}, u32[]{:S(2)}, u32[]{:S(2)}) collective-permute-start(bf16[128,2688]{1,0:T(8,128)(2,1)} %fusion.6), channel_id=1, source_target_pairs={{0,1},{1,0},{2,3},{3,2},{4,5},{5,4},{6,7},{7,6},{8,9},{9,8},{10,11... | collective-permute-start | bytes 2064392 | tf_op jit(solution)/shard_map/ppermute | solution.py:19
Sparse Core Ops, SparseCore 0:
  10.3 106.6 all-gather.2
  150.2 71.1 all-gather.4

commit v2 on v1

--- a/solution.py
+++ b/solution.py
@@ -1,6 +1,10 @@
+import functools
+
 import jax
 import jax.numpy as jnp
 from jax import lax
+from jax.experimental import pallas as pl
+from jax.experimental.pallas import tpu as pltpu
 from jax.sharding import PartitionSpec as P
 
 WINDOW_TOKENS = 1024
@@ -21,6 +25,181 @@
 
 def matmul(a, b, dims):
     return lax.dot_general(a, b, (dims, ((), ())), preferred_element_type=F32)
+
+
+def ring_place(position, count):
+    half = count // 2
+    down = position // half
+    step = lax.rem(position, half)
+    pair, core = step // 2, lax.rem(step, 2)
+    level = pair + down * (half // 2 - 1 - 2 * pair)
+    return level * 4 + down * 2 + core
+
+
+def ring_position(index, count):
+    half = count // 2
+    level, down, core = index // 4, lax.rem(index // 2, 2), lax.rem(index, 2)
+    pair = level + down * (half // 2 - 1 - 2 * level)
+    return down * half + pair * 2 + core
+
+
+def ring_kernel(
+    count,
+    grad_ref,
+    proj_ref,
+    att_ref,
+    all_ref,
+    sum_ref,
+    out_right,
+    out_left,
+    in_right,
+    in_left,
+    gr_send,
+    gr_recv,
+    gl_send,
+    gl_recv,
+    sr_send,
+    sr_recv,
+    sl_send,
+    sl_recv,
+):
+    me = lax.axis_index("ctx")
+    here = ring_position(me, count)
+    hops_right = count // 2
+    hops_left = count - 1 - hops_right
+
+    def place(offset):
+        return ring_place(lax.rem(here + offset + count, count), count)
+
+    right, left = {"ctx": place(1)}, {"ctx": place(-1)}
+    barrier = pltpu.get_barrier_semaphore()
+    for neighbour in (left, right):
+        pl.semaphore_signal(
+            barrier, inc=1, device_id=neighbour, device_id_type=pl.DeviceIdType.MESH
+        )
+    pl.semaphore_wait(barrier, 2)
+
+    def remote(src, dst, send, recv, target):
+        return pltpu.make_async_remote_copy(
+            src_ref=src,
+            dst_ref=dst,
+            send_sem=send,
+            recv_sem=recv,
+            device_id=target,
+            device_id_type=pl.DeviceIdType.MESH,
+        )
+
+    def gather_right(s):
+        slot = all_ref.at[place(-s)]
+        return remote(slot, slot, gr_send.at[s], gr_recv.at[s], right)
+
+    def gather_left(s):
+        slot = all_ref.at[place(s)]
+        return remote(slot, slot, gl_send.at[s], gl_recv.at[s], left)
+
+    def sum_right(s):
+        return remote(out_right.at[s], in_right.at[s], sr_send.at[s], sr_recv.at[s], right)
+
+    def sum_left(s):
+        return remote(out_left.at[s], in_left.at[s], sl_send.at[s], sl_recv.at[s], left)
+
+    def arrived_right(s):
+        slot = all_ref.at[place(-s - 1)]
+        return remote(slot, slot, gr_send.at[s], gr_recv.at[s], right)
+
+    def arrived_left(s):
+        slot = all_ref.at[place(s + 1)]
+        return remote(slot, slot, gl_send.at[s], gl_recv.at[s], left)
+
+    def term(offset):
+        return jnp.dot(grad_ref[place(offset)], proj_ref[...], preferred_element_type=F32)
+
+    all_ref[me] = att_ref[...]
+
+    def step(s, first, both):
+        own = term(hops_right - s)
+        if not first:
+            sum_right(s - 1).wait_recv()
+            own = own + in_right[s - 1].astype(F32)
+        out_right[s] = own.astype(BF16)
+        sum_right(s).start()
+        if both:
+            own = term(s - hops_left)
+            if not first:
+                sum_left(s - 1).wait_recv()
+                own = own + in_left[s - 1].astype(F32)
+            out_left[s] = own.astype(BF16)
+            sum_left(s).start()
+        if not first:
+            arrived_right(s - 1).wait_recv()
+        gather_right(s).start()
+        if both:
+            if not first:
+                arrived_left(s - 1).wait_recv()
+            gather_left(s).start()
+
+    def middle(s, carry):
+        step(s, False, True)
+        return carry
+
+    step(0, True, True)
+    lax.fori_loop(1, hops_left, middle, 0)
+    step(hops_left, False, False)
+
+    own = term(0)
+    sum_left(hops_left - 1).wait_recv()
+    own = own + in_left[hops_left - 1].astype(F32)
+    sum_right(hops_right - 1).wait_recv()
+    own = own + in_right[hops_right - 1].astype(F32)
+    sum_ref[...] = own.astype(BF16)
+    arrived_left(hops_left - 1).wait_recv()
+    arrived_right(hops_right - 1).wait_recv()
+
+    def drain_left(s, carry):
+        sum_left(s).wait_send()
+        gather_left(s).wait_send()
+        return carry
+
+    def drain_right(s, carry):
+        sum_right(s).wait_send()
+        gather_right(s).wait_send()
+        return carry
+
+    lax.fori_loop(0, hops_left, drain_left, 0)
+    lax.fori_loop(0, hops_right, drain_right, 0)
+
+
+def ring(grad_blocks, proj, attended):
+    count, tok_rows, depth = grad_blocks.shape
+    width = attended.shape[1]
+    right = count // 2
+    left = count - 1 - right
+    vmem = pl.BlockSpec(memory_space=pltpu.VMEM)
+    dma = pltpu.SemaphoreType.DMA
+    return pl.pallas_call(
+        functools.partial(ring_kernel, count),
+        out_shape=(
+            jax.ShapeDtypeStruct((count, tok_rows, width), BF16),
+            jax.ShapeDtypeStruct((tok_rows, width), BF16),
+        ),
+        in_specs=[vmem] * 3,
+        out_specs=(vmem, vmem),
+        scratch_shapes=[
+            pltpu.VMEM((right, tok_rows, width), BF16),
+            pltpu.VMEM((left, tok_rows, width), BF16),
+            pltpu.VMEM((right, tok_rows, width), BF16),
+            pltpu.VMEM((left, tok_rows, width), BF16),
+        ]
+        + [dma((right,)), dma((right,)), dma((left,)), dma((left,))] * 2,
+        compiler_params=pltpu.CompilerParams(
+            collective_id=0, has_side_effects=True, vmem_limit_bytes=48 << 20
+        ),
+        cost_estimate=pl.CostEstimate(
+            flops=2 * count * tok_rows * depth * width,
+            bytes_accessed=4 * count * tok_rows * width,
+            transcendentals=0,
+        ),
+    )(grad_blocks, proj, attended)
 
 
 def shards(queries, rotated_keys, value_vectors, out_grad, out_proj, seg_ids):
@@ -54,8 +233,6 @@
     kv = jnp.concatenate(received[::-1] + [own_kv], axis=0)
     keys, values = kv[:, :head_size], kv[:, head_size:]
 
-    proj_full = lax.all_gather(out_proj, "ctx", axis=0, tiled=True)
-
     columns = out_grad.shape[1]
     grad_full = jnp.zeros((tok_rows, columns * head_count), BF16)
     grad_full = lax.dynamic_update_slice_in_dim(grad_full, out_grad, head_index * columns, 1)
@@ -84,19 +261,25 @@
     probs_bf = probs.astype(BF16)
     attended = jnp.einsum("hts,sd->htd", probs_bf, values, preferred_element_type=F32).astype(BF16)
     attended_tok = to_tokens(attended.transpose(1, 0, 2).reshape(rows, q_width))
-    attended_all = lax.all_gather(attended_tok, "ctx", axis=0, tiled=True)
-
-    grad_att_tok = matmul(grad_full, proj_full, ((1,), (0,))).astype(BF16)
+
+    proj_rows = out_proj.shape[0]
+    pad = -proj_rows % 128
+    grad_blocks = grad_columns.reshape(ctx_count, tok_rows, proj_rows)
+    attended_all, grad_att_tok = ring(
+        jnp.pad(grad_blocks, ((0, 0), (0, 0), (0, pad))),
+        jnp.pad(out_proj, ((0, pad), (0, 0))),
+        attended_tok,
+    )
+    attended_all = attended_all.reshape(ctx_count * tok_rows, heads_query * head_size)
     grad_att = to_heads(grad_att_tok).reshape(rows, per_kv, head_size).transpose(1, 0, 2)
 
-    def out_columns(which):
-        block = lax.dynamic_slice_in_dim(proj_full, which * columns, columns, 0)
-        return matmul(attended_tok, block, ((1,), (1,)))
-
-    layer_out = out_columns(head_index)
+    out_part = matmul(attended_all, out_proj, ((1,), (1,))).astype(BF16)
+    out_part = lax.all_to_all(out_part, "ctx", 0, 1, tiled=True)
+    layer_out = lax.dynamic_slice_in_dim(out_part, head_index * columns, columns, 1).astype(F32)
     for d in range(1, head_count):
         target = lax.rem(head_index + d, head_count)
-        layer_out = layer_out + rotated(out_columns(target).astype(BF16), "head", d).astype(F32)
+        block = lax.dynamic_slice_in_dim(out_part, target * columns, columns, 1)
+        layer_out = layer_out + rotated(block, "head", d).astype(F32)
     layer_out = layer_out.astype(BF16)
 
     grad_proj = matmul(grad_columns, attended_all, ((0,), (0,))) * (ctx_count * tok_rows) ** (-0.5)

time: 250 us -> 245 us (0.980); the launches traced: 246 us -> 244 us
  Pallas kernels: 0 us -> 52 us
  waiting for transfers between devices: 120 us -> 90.7 us
  blocking collectives: 26.3 us -> 0 us
  starting transfers between devices: 27.2 us -> 48.6 us
  matrix products: 36.3 us -> 22 us
  between operations: 14.3 us -> 1.08 us
  local copies, waits for them, and re-layouts: 15.8 us -> 21.4 us
    all_gather x2 -> x0, waiting for transfers between devices: 56.4 us -> none  [the longest x1 56.4 us: shards(): proj_full = lax.all_gather(out_proj, 'ctx', axis=0, tiled=True)]
    pallas_call x0 -> x1, Pallas kernels: none -> 52 us  [ring(): pl.pallas_call(functools.partial(ring_kernel, count), out_shape=(jax.Shap...]
    all_to_all x1, waiting for transfers between devices: 0.01 us -> 28.5 us  [shards(): grad_columns = lax.all_to_all(grad_full, 'ctx', 1, 0, tiled=True)]
    all_to_all x2 -> x0, blocking collectives: 26.3 us -> none  [to_tokens(): lax.all_to_all(value, 'ctx', 0, 1, axis_index_groups=groups, tiled=True)]
    dot_general x4 -> x2, matrix products: 21.7 us -> 9.08 us  [matmul(): return lax.dot_general(a, b, (dims, ((), ())), preferred_element_type=F32)]
    all_to_all x0 -> x3, starting transfers between devices: none -> 12.5 us  [the longest x2 6.88 us: to_tokens(): lax.all_to_all(value, 'ctx', 0, 1, axis_index_groups=groups, tiled=True)]
    all_to_all x1, starting transfers between devices: 3.7 us -> 11.4 us  [shards(): grad_columns = lax.all_to_all(grad_full, 'ctx', 1, 0, tiled=True)]
    ppermute x2, waiting for transfers between devices: 13.6 us -> 7.42 us  [rotated(): lax.ppermute(value, axis, [(i, (i + by) % count) for i in range(count)])]
  transfers between devices with their start and end apart: 11 -> 12, of which waited for: 8 -> 10; matrix products, arithmetic and copies ran while one was open for 15% -> 16% of each run, Pallas kernels for 0% -> 0%
where the time goes in v2:
time: 245 us; the launch traced here: 244 us
  waiting for transfers between devices  90.7 us (37%)
  Pallas kernels  52 us (21%)
  starting transfers between devices  48.6 us (20%)
  matrix products  22 us (9%)
  local copies, waits for them, and re-layouts  21.4 us (9%)
  other arithmetic  8.15 us (3%)
    pallas_call x1, Pallas kernels, ring(): pl.pallas_call(functools.partial(ring_kernel, count), out_shape=(jax.Shap...  52 us
    ppermute x4, waiting for transfers between devices, shifted(): return lax.ppermute(value, axis, pairs)  43.1 us
    all_to_all x1, waiting for transfers between devices, shards(): grad_columns = lax.all_to_all(grad_full, 'ctx', 1, 0, tiled=True)  28.5 us
    all_to_all x1, starting transfers between devices, shards(): grad_columns = lax.all_to_all(grad_full, 'ctx', 1, 0, tiled=True)  11.4 us
    ppermute x4, starting transfers between devices, shifted(): return lax.ppermute(value, axis, pairs)  11.4 us
    all_to_all x2, starting transfers between devices, to_heads(): lax.all_to_all(value, 'ctx', 1, 0, axis_index_groups=groups, tiled=True)  9.49 us
    dot_general x2, matrix products, matmul(): return lax.dot_general(a, b, (dims, ((), ())), preferred_element_type=F32)  9.08 us
    unnamed x36, local copies, waits for them, and re-layouts  8.24 us
  transfers between devices with their start and end apart: 12, of which 10 were waited for; matrix products, arithmetic and copies ran while one was open for 16% of the time, Pallas kernels for 0%

profile of v2, /device:TPU:0, one launch (start us, length us, event | category | flops | bytes accessed | tf_op | source)
XLA Modules:
  0.0 243.9 jit_solution(16853221787420030480)
XLA Ops:
  0.7 1.0 copy.69
  1.6 0.9 copy.70
  2.6 1.1 reshape.72
  3.7 0.8 pad_maximum_fusion.2
  4.6 4.2 %all-to-all-start.1 = ((bf16[128,4,512]{2,0,1:T(8,128)(2,1)}), bf16[128,4,512]{2,0,1:T(8,128)(2,1)S(1)}, u32[]{:S(2)}, u32[]{:S(2)}) async-start(bf16[128,4,512]{2,0,1:T(8,128)(2,1)} %pad_maximum_fusion.2), calls=%async_computation.1 | async-start | bytes 1048576 | tf_op jit(solution)/shard_map/all_to_all | solution.py:221
  9.2 2.3 collective-permute-start
  11.6 1.2 fusion.6
  12.8 4.9 %all-to-all-done.1 = bf16[128,4,512]{2,0,1:T(8,128)(2,1)S(1)} async-done(((bf16[128,4,512]{2,0,1:T(8,128)(2,1)}), bf16[128,4,512]{2,0,1:T(8,128)(2,1)S(1)}, u32[]{:S(2)}, u32[]{:S(2)}) %all-to-all-start.1) | async-done | bytes 524320 | tf_op jit(solution)/shard_map/all_to_all | solution.py:221
  17.7 4.2 %collective-permute-start.2 = (bf16[512,256]{1,0:T(8,128)(2,1)S(1)}, bf16[512,256]{1,0:T(8,128)(2,1)S(1)}, u32[]{:S(2)}, u32[]{:S(2)}) collective-permute-start(bf16[512,256]{1,0:T(8,128)(2,1)S(1)} %get-tuple-element.29), channel_id=1, source_target_pairs={{0,8},{2,10},{4,12},{6,14},{8,16},{10,18},{12,20},{14,22},{16,24},... | collective-permute-start | bytes 786440 | tf_op jit(solution)/shard_map/ppermute | solution.py:18
  21.9 4.5 %collective-permute-start.1 = (bf16[512,256]{1,0:T(8,128)(2,1)S(1)}, bf16[512,256]{1,0:T(8,128)(2,1)S(1)}, u32[]{:S(2)}, u32[]{:S(2)}) collective-permute-start(bf16[512,256]{1,0:T(8,128)(2,1)S(1)} %get-tuple-element.29), channel_id=1, source_target_pairs={{0,16},{2,18},{4,20},{6,22},{8,24},{10,26},{12,28},{14,30},{1,17},... | collective-permute-start | bytes 786440 | tf_op jit(solution)/shard_map/ppermute | solution.py:18
  26.4 1.3 broadcast_in_dim.14
  27.6 0.9 constant_dynamic-update-slice_fusion.1
  28.6 4.3 %collective-permute-done.1 = bf16[512,256]{1,0:T(8,128)(2,1)S(1)} collective-permute-done((bf16[512,256]{1,0:T(8,128)(2,1)S(1)}, bf16[512,256]{1,0:T(8,128)(2,1)S(1)}, u32[]{:S(2)}, u32[]{:S(2)}) %collective-permute-start.1) | collective-permute-done | bytes 262176 | tf_op jit(solution)/shard_map/ppermute | solution.py:18
  32.9 5.7 %fusion.33 = (f32[2,512]{1,0:T(2,128)S(1)}, f32[2,512,1536]{2,1,0:T(8,128)}) fusion(pred[512,1536]{1,0:T(8,128)(4,1)S(1)} %fusion.6, bf16[1536,256]{1,0:T(8,128)(2,1)S(1)} %pad_maximum_fusion.1, bf16[64,2,8,128]{3,2,1,0:T(8,128)(2,1)S(1)} %get-tuple-element.28), kind=kOutput, calls=%fused_computation.63 | convolution fusion | flops 410519040 | bytes 8523776 | tf_op jit(solution)/shard_map/sub | solution.py:259
  38.7 3.6 %fusion.8 = bf16[2,512,1536]{2,1,0:T(8,128)(2,1)S(1)} fusion(f32[2,512,1536]{2,1,0:T(8,128)} %get-tuple-element.31, f32[2,512]{1,0:T(2,128)S(1)} %get-tuple-element.30), kind=kLoop, calls=%fused_computation.14 | loop fusion | flops 3145728 | bytes 9441280 | tf_op jit(solution)/shard_map/convert_element_type | solution.py:261
  42.3 1.8 copy-done
  44.0 1.2 convolution_convert_fusion.1
  45.3 0.9 copy.73
  46.2 3.4 %all-to-all-start.2 = ((bf16[4,128,256]{2,1,0:T(8,128)(2,1)}), bf16[4,128,256]{2,1,0:T(8,128)(2,1)S(1)}, u32[]{:S(2)}, u32[]{:S(2)}) async-start(bf16[4,128,256]{2,1,0:T(8,128)(2,1)} %copy.73), calls=%async_computation.2 | async-start | bytes 524288 | tf_op jit(solution)/shard_map/all_to_all | solution.py:224
  49.6 0.9 constant_dynamic-update-slice_fusion
  50.5 5.1 %all-to-all-done.2 = bf16[4,128,256]{2,1,0:T(8,128)(2,1)S(1)} async-done(((bf16[4,128,256]{2,1,0:T(8,128)(2,1)}), bf16[4,128,256]{2,1,0:T(8,128)(2,1)S(1)}, u32[]{:S(2)}, u32[]{:S(2)}) %all-to-all-start.2) | async-done | bytes 262176 | tf_op jit(solution)/shard_map/all_to_all | solution.py:224
  55.6 11.4 %all-to-all-start = ((bf16[128,16,336]{0,2,1:T(8,128)(2,1)}), bf16[128,16,336]{0,2,1:T(8,128)(2,1)}, u32[]{:S(2)}, u32[]{:S(2)}) async-start(bf16[128,16,336]{0,2,1:T(8,128)(2,1)} %bitcast), calls=%async_computation | async-start | bytes 2752512 | tf_op jit(solution)/shard_map/all_to_all | solution.py:243
  67.1 28.5 %all-to-all-done = bf16[128,16,336]{0,2,1:T(8,128)(2,1)} async-done(((bf16[128,16,336]{0,2,1:T(8,128)(2,1)}), bf16[128,16,336]{0,2,1:T(8,128)(2,1)}, u32[]{:S(2)}, u32[]{:S(2)}) %all-to-all-start) | async-done | bytes 1376288 | tf_op jit(solution)/shard_map/all_to_all | solution.py:243
  95.6 1.8 copy.67
  97.7 52.0 %shard_map.101 = (bf16[16,128,1024]{2,1,0:T(8,128)(2,1)}, bf16[128,1024]{1,0:T(8,128)(2,1)S(1)}) custom-call(bf16[16,128,384]{2,1,0:T(8,128)(2,1)S(1)} %pad.9.grad_ref, bf16[384,1024]{1,0:T(8,128)(2,1)S(1)} %pad.10.proj_ref, bf16[128,1024]{1,0:T(8,128)(2,1)S(1)} %bitcast.100), custom_call_target="tpu_custom_call" | custom-call | flops 1610612736 | bytes 8388608 | tf_op jit(solution)/shard_map/pallas_call | solution.py:179
  150.5 5.3 %all-to-all-start.4 = ((bf16[128,4,256]{2,0,1:T(8,128)(2,1)}), bf16[128,4,256]{2,0,1:T(8,128)(2,1)S(1)}, u32[]{:S(2)}, u32[]{:S(2)}) async-start(bf16[128,4,256]{2,0,1:T(8,128)(2,1)} %bitcast.99), calls=%async_computation.4 | async-start | bytes 524288 | tf_op jit(solution)/shard_map/all_to_all | solution.py:221
  155.7 3.8 %fusion.11 = bf16[42,16,8,128]{3,2,1,0:T(8,128)(2,1)S(1)} fusion(bf16[2048,1024]{1,0:T(8,128)(2,1)} %bitcast.112, bf16[336,1024]{1,0:T(8,128)(2,1)S(1)} %copy-done.12), kind=kOutput, calls=%fused_computation.22 | convolution fusion | flops 1409974272 | bytes 6258688 | tf_op jit(solution)/shard_map/dot_general | solution.py:27
  159.6 1.3 copy.125
  160.9 0.9 all-to-all-done.4
  161.8 5.7 %all-to-all-start.3 = ((bf16[16,128,336]{1,2,0:T(8,128)(2,1)}), bf16[16,128,336]{1,2,0:T(8,128)(2,1)}, u32[]{:S(2)}, u32[]{:S(2)}) async-start(bf16[16,128,336]{1,2,0:T(8,128)(2,1)} %bitcast.103), calls=%async_computation.3 | async-start | bytes 2752512 | tf_op jit(solution)/shard_map/all_to_all | solution.py:277
  168.2 1.1 copy.98
  170.6 3.6 %multiply_convert_fusion = bf16[2,512,1536]{2,1,0:T(8,128)(2,1)S(1)} fusion(f32[2,512]{1,0:T(2,128)S(1)} %multiply_reduce_fusion, f32[2,512,1536]{2,1,0:T(8,128)} %get-tuple-element.31, f32[2,512]{1,0:T(2,128)S(1)} %get-tuple-element.30, bf16[1536,256]{1,0:T(8,128)(2,1)S(1)} %copy-done.5, bf16[512,2,128]{0,2,1:T(8,128)(2,1)S(1)} %copy.98), kind=kOutput, calls=%fused_computation.1 | convolution fusion | flops 408944640 | bytes 10100736 | tf_op jit(solution)/shard_map/htd,sd->hts/dot_general | solution.py:287
  175.0 1.4 collective-permute-start.4
  176.4 1.3 collective-permute-start.5
  177.7 1.2 fusion.15
  179.2 19.1 %collective-permute-done.4 = bf16[512,256]{0,1:T(8,128)(2,1)S(1)} collective-permute-done((bf16[512,256]{0,1:T(8,128)(2,1)S(1)}, bf16[512,256]{0,1:T(8,128)(2,1)S(1)}, u32[]{:S(2)}, u32[]{:S(2)}) %collective-permute-start.4) | collective-permute-done | bytes 262176 | tf_op jit(solution)/shard_map/ppermute | solution.py:18
  198.3 19.6 %collective-permute-done.5 = bf16[512,256]{0,1:T(8,128)(2,1)S(1)} collective-permute-done((bf16[512,256]{0,1:T(8,128)(2,1)S(1)}, bf16[512,256]{0,1:T(8,128)(2,1)S(1)}, u32[]{:S(2)}, u32[]{:S(2)}) %collective-permute-start.5) | collective-permute-done | bytes 262176 | tf_op jit(solution)/shard_map/ppermute | solution.py:18
  218.2 0.8 pad_maximum_fusion.3
  219.0 3.5 %all-to-all-start.5 = ((bf16[4,128,512]{2,1,0:T(8,128)(2,1)}), bf16[4,128,512]{2,1,0:T(8,128)(2,1)S(1)}, u32[]{:S(2)}, u32[]{:S(2)}) async-start(bf16[4,128,512]{2,1,0:T(8,128)(2,1)} %pad_maximum_fusion.3), calls=%async_computation.5 | async-start | bytes 1048576 | tf_op jit(solution)/shard_map/all_to_all | solution.py:224
  222.5 1.2 constant_dynamic-slice_fusion
  223.6 1.6 collective-permute-start.3
  225.2 5.3 %fusion.12 = f32[336,1024]{1,0:T(8,128)} fusion(bf16[16,128,1024]{2,1,0:T(8,128)(2,1)} %get-tuple-element.7, bf16[128,16,336]{0,2,1:T(8,128)(2,1)} %all-to-all-done), kind=kOutput, calls=%fused_computation.24 | convolution fusion | flops 1409630208 | bytes 6946816 | tf_op jit(solution)/shard_map/dot_general | solution.py:27
  230.5 0.8 all-to-all-done.5
  231.6 0.8 copy.88
  232.4 0.9 copy.86
  234.1 7.4 %collective-permute-done.3 = bf16[128,2688]{0,1:T(8,128)(2,1)S(1)} collective-permute-done((bf16[128,2688]{0,1:T(8,128)(2,1)S(1)}, bf16[128,2688]{0,1:T(8,128)(2,1)S(1)}, u32[]{:S(2)}, u32[]{:S(2)}) %collective-permute-start.3) | collective-permute-done | bytes 688160 | tf_op jit(solution)/shard_map/ppermute | solution.py:23
  241.5 1.3 add_convert_fusion
  242.8 1.1 copy.85
  (57 shorter events, 6.1 us)
Async XLA Ops:
  0.6 8.2 %copy-start.10 = (bf16[128,2688]{1,0:T(8,128)(2,1)S(1)}, bf16[128,2688]{1,0:T(8,128)(2,1)}, u32[]{:S(2)}) copy-start(bf16[128,2688]{1,0:T(8,128)(2,1)} %param.9) | copy-start | bytes 2064388
  0.6 10.8 %copy-start.13 = (s32[2048]{0:T(1024)S(1)}, s32[2048]{0:T(1024)}, u32[]{:S(2)}) copy-start(s32[2048]{0:T(1024)} %param.11) | copy-start | bytes 24580
  4.6 13.1 %all-to-all-start.1 = ((bf16[128,4,512]{2,0,1:T(8,128)(2,1)}), bf16[128,4,512]{2,0,1:T(8,128)(2,1)S(1)}, u32[]{:S(2)}, u32[]{:S(2)}) async-start(bf16[128,4,512]{2,0,1:T(8,128)(2,1)} %pad_maximum_fusion.2), calls=%async_computation.1 | async-start | bytes 1048576 | tf_op jit(solution)/shard_map/all_to_all | solution.py:221
  9.2 40.4 %collective-permute-start = (bf16[128,2688]{0,1:T(8,128)(2,1)S(1)}, bf16[128,2688]{0,1:T(8,128)(2,1)S(1)}, u32[]{:S(2)}, u32[]{:S(2)}) collective-permute-start(bf16[128,2688]{0,1:T(8,128)(2,1)S(1)} %copy.65), channel_id=1, source_target_pairs={{0,1},{1,0},{2,3},{3,2},{4,5},{5,4},{6,7},{7,6},{8,9},{9,8},{10,11... | collective-permute-start | bytes 2064392 | tf_op jit(solution)/shard_map/ppermute | solution.py:23
  17.7 21.0 %copy-start.8 = (bf16[64,2,8,128]{3,2,1,0:T(8,128)(2,1)}, bf16[64,2,8,128]{3,2,1,0:T(8,128)(2,1)S(1)}, u32[]{:S(2)}) copy-start(bf16[64,2,8,128]{3,2,1,0:T(8,128)(2,1)S(1)} %get-tuple-element.28) | copy-start | bytes 786436
  17.7 10.9 %collective-permute-start.2 = (bf16[512,256]{1,0:T(8,128)(2,1)S(1)}, bf16[512,256]{1,0:T(8,128)(2,1)S(1)}, u32[]{:S(2)}, u32[]{:S(2)}) collective-permute-start(bf16[512,256]{1,0:T(8,128)(2,1)S(1)} %get-tuple-element.29), channel_id=1, source_target_pairs={{0,8},{2,10},{4,12},{6,14},{8,16},{10,18},{12,20},{14,22},{16,24},... | collective-permute-start | bytes 786440 | tf_op jit(solution)/shard_map/ppermute | solution.py:18
  21.9 11.0 %collective-permute-start.1 = (bf16[512,256]{1,0:T(8,128)(2,1)S(1)}, bf16[512,256]{1,0:T(8,128)(2,1)S(1)}, u32[]{:S(2)}, u32[]{:S(2)}) collective-permute-start(bf16[512,256]{1,0:T(8,128)(2,1)S(1)} %get-tuple-element.29), channel_id=1, source_target_pairs={{0,16},{2,18},{4,20},{6,22},{8,24},{10,26},{12,28},{14,30},{1,17},... | collective-permute-start | bytes 786440 | tf_op jit(solution)/shard_map/ppermute | solution.py:18
  32.9 9.3 %copy-start.4 = (bf16[1536,256]{1,0:T(8,128)(2,1)}, bf16[1536,256]{1,0:T(8,128)(2,1)S(1)}, u32[]{:S(2)}) copy-start(bf16[1536,256]{1,0:T(8,128)(2,1)S(1)} %pad_maximum_fusion.1) | copy-start | bytes 2359300
  42.3 1.8 copy-start
  45.2 21.9 %copy-start.6 = (bf16[2,512,128]{1,2,0:T(8,128)(2,1)}, bf16[2,512,128]{1,2,0:T(8,128)(2,1)S(1)}, u32[]{:S(2)}) copy-start(bf16[2,512,128]{1,2,0:T(8,128)(2,1)S(1)} %convolution_convert_fusion.1) | copy-start | bytes 786436
  45.2 21.8 %copy-start.11 = (bf16[336,1024]{1,0:T(8,128)(2,1)S(1)}, bf16[336,1024]{1,0:T(8,128)(2,1)}, u32[]{:S(2)}) copy-start(bf16[336,1024]{1,0:T(8,128)(2,1)} %param.10) | copy-start | bytes 2064388
  46.2 9.4 %all-to-all-start.2 = ((bf16[4,128,256]{2,1,0:T(8,128)(2,1)}), bf16[4,128,256]{2,1,0:T(8,128)(2,1)S(1)}, u32[]{:S(2)}, u32[]{:S(2)}) async-start(bf16[4,128,256]{2,1,0:T(8,128)(2,1)} %copy.73), calls=%async_computation.2 | async-start | bytes 524288 | tf_op jit(solution)/shard_map/all_to_all | solution.py:224
  55.6 40.0 %all-to-all-start = ((bf16[128,16,336]{0,2,1:T(8,128)(2,1)}), bf16[128,16,336]{0,2,1:T(8,128)(2,1)}, u32[]{:S(2)}, u32[]{:S(2)}) async-start(bf16[128,16,336]{0,2,1:T(8,128)(2,1)} %bitcast), calls=%async_computation | async-start | bytes 2752512 | tf_op jit(solution)/shard_map/all_to_all | solution.py:243
  97.7 58.0 %copy-start.12 = (bf16[336,1024]{1,0:T(8,128)(2,1)S(1)}, bf16[336,1024]{1,0:T(8,128)(2,1)}, u32[]{:S(2)}) copy-start(bf16[336,1024]{1,0:T(8,128)(2,1)} %param.10) | copy-start | bytes 2064388
  150.5 11.3 %all-to-all-start.4 = ((bf16[128,4,256]{2,0,1:T(8,128)(2,1)}), bf16[128,4,256]{2,0,1:T(8,128)(2,1)S(1)}, u32[]{:S(2)}, u32[]{:S(2)}) async-start(bf16[128,4,256]{2,0,1:T(8,128)(2,1)} %bitcast.99), calls=%async_computation.4 | async-start | bytes 524288 | tf_op jit(solution)/shard_map/all_to_all | solution.py:221
  159.6 9.8 %copy-start.1 = (bf16[2,512,1536]{2,1,0:T(8,128)(2,1)S(1)}, bf16[2,512,1536]{2,1,0:T(8,128)(2,1)}, u32[]{:S(2)}) copy-start(bf16[2,512,1536]{2,1,0:T(8,128)(2,1)} %copy-done) | copy-start | bytes 9437188
  161.8 57.2 %all-to-all-start.3 = ((bf16[16,128,336]{1,2,0:T(8,128)(2,1)}), bf16[16,128,336]{1,2,0:T(8,128)(2,1)}, u32[]{:S(2)}, u32[]{:S(2)}) async-start(bf16[16,128,336]{1,2,0:T(8,128)(2,1)} %bitcast.103), calls=%async_computation.3 | async-start | bytes 2752512 | tf_op jit(solution)/shard_map/all_to_all | solution.py:277
  169.3 1.0 copy-start.7
  169.3 1.2 copy-start.5
  170.3 4.5 %copy-start.2 = (f32[1536,128]{0,1:T(8,128)}, f32[1536,128]{0,1:T(8,128)S(1)}, u32[]{:S(2)}) copy-start(f32[1536,128]{0,1:T(8,128)S(1)} %convolution_bitcast_fusion) | copy-start | bytes 2359300
  170.6 3.6 %copy-start.9 = (bf16[64,2,8,128]{3,2,1,0:T(8,128)(2,1)S(1)}, bf16[64,2,8,128]{3,2,1,0:T(8,128)(2,1)}, u32[]{:S(2)}) copy-start(bf16[64,2,8,128]{3,2,1,0:T(8,128)(2,1)} %copy-done.8) | copy-start | bytes 786436
  174.9 43.0 %copy-start.3 = (f32[1536,128]{0,1:T(8,128)S(1)}, f32[1536,128]{0,1:T(8,128)}, u32[]{:S(2)}) copy-start(f32[1536,128]{0,1:T(8,128)} %copy-done.2) | copy-start | bytes 2359300
  175.0 23.3 %collective-permute-start.4 = (bf16[512,256]{0,1:T(8,128)(2,1)S(1)}, bf16[512,256]{0,1:T(8,128)(2,1)S(1)}, u32[]{:S(2)}, u32[]{:S(2)}) collective-permute-start(bf16[512,256]{0,1:T(8,128)(2,1)S(1)} %get-tuple-element.24), channel_id=1, source_target_pairs={{8,0},{10,2},{12,4},{14,6},{16,8},{18,10},{20,12},{22,14},{24,16},... | collective-permute-start | bytes 786440 | tf_op jit(solution)/shard_map/ppermute | solution.py:18
  176.4 41.5 %collective-permute-start.5 = (bf16[512,256]{0,1:T(8,128)(2,1)S(1)}, bf16[512,256]{0,1:T(8,128)(2,1)S(1)}, u32[]{:S(2)}, u32[]{:S(2)}) collective-permute-start(bf16[512,256]{0,1:T(8,128)(2,1)S(1)} %get-tuple-element.25), channel_id=1, source_target_pairs={{16,0},{18,2},{20,4},{22,6},{24,8},{26,10},{28,12},{30,14},{17,1},... | collective-permute-start | bytes 786440 | tf_op jit(solution)/shard_map/ppermute | solution.py:18
  219.0 12.3 %all-to-all-start.5 = ((bf16[4,128,512]{2,1,0:T(8,128)(2,1)}), bf16[4,128,512]{2,1,0:T(8,128)(2,1)S(1)}, u32[]{:S(2)}, u32[]{:S(2)}) async-start(bf16[4,128,512]{2,1,0:T(8,128)(2,1)} %pad_maximum_fusion.3), calls=%async_computation.5 | async-start | bytes 1048576 | tf_op jit(solution)/shard_map/all_to_all | solution.py:224
  223.6 17.9 %collective-permute-start.3 = (bf16[128,2688]{0,1:T(8,128)(2,1)S(1)}, bf16[128,2688]{0,1:T(8,128)(2,1)S(1)}, u32[]{:S(2)}, u32[]{:S(2)}) collective-permute-start(bf16[128,2688]{0,1:T(8,128)(2,1)S(1)} %constant_dynamic-slice_fusion), channel_id=1, source_target_pairs={{0,1},{1,0},{2,3},{3,2},{4,5},{5,4},{6,7},{7,6},{8,9},{9,8},{10,11... | collective-permute-start | bytes 2064392 | tf_op jit(solution)/shard_map/ppermute | solution.py:23

commit v3 on v1

--- a/solution.py
+++ b/solution.py
@@ -1,6 +1,10 @@
+import functools
+
 import jax
 import jax.numpy as jnp
 from jax import lax
+from jax.experimental import pallas as pl
+from jax.experimental.pallas import tpu as pltpu
 from jax.sharding import PartitionSpec as P
 
 WINDOW_TOKENS = 1024
@@ -21,6 +25,201 @@
 
 def matmul(a, b, dims):
     return lax.dot_general(a, b, (dims, ((), ())), preferred_element_type=F32)
+
+
+def ring_place(position, count):
+    half = count // 2
+    down = position // half
+    step = lax.rem(position, half)
+    pair, core = step // 2, lax.rem(step, 2)
+    level = pair + down * (half // 2 - 1 - 2 * pair)
+    return level * 4 + down * 2 + core
+
+
+def ring_position(index, count):
+    half = count // 2
+    level, down, core = index // 4, lax.rem(index // 2, 2), lax.rem(index, 2)
+    pair = level + down * (half // 2 - 1 - 2 * level)
+    return down * half + pair * 2 + core
+
+
+def neighbours(count):
+    here = ring_position(lax.axis_index("ctx"), count)
+
+    def place(offset):
+        return ring_place(lax.rem(here + offset + count, count), count)
+
+    right, left = {"ctx": place(1)}, {"ctx": place(-1)}
+    barrier = pltpu.get_barrier_semaphore()
+    for neighbour in (left, right):
+        pl.semaphore_signal(
+            barrier, inc=1, device_id=neighbour, device_id_type=pl.DeviceIdType.MESH
+        )
+    pl.semaphore_wait(barrier, 2)
+    return place, right, left
+
+
+def remote(src, dst, sems, s, target):
+    send, recv = sems
+    return pltpu.make_async_remote_copy(
+        src_ref=src,
+        dst_ref=dst,
+        send_sem=send.at[s],
+        recv_sem=recv.at[s],
+        device_id=target,
+        device_id_type=pl.DeviceIdType.MESH,
+    )
+
+
+def gather_kernel(count, own_ref, all_ref, r_send, r_recv, l_send, l_recv):
+    hops_right = count // 2
+    hops_left = count - 1 - hops_right
+    place, right, left = neighbours(count)
+
+    def block_right(s, sem):
+        slot = all_ref.at[place(-s)]
+        return remote(slot, slot, (r_send, r_recv), sem, right)
+
+    def block_left(s, sem):
+        slot = all_ref.at[place(s)]
+        return remote(slot, slot, (l_send, l_recv), sem, left)
+
+    all_ref[lax.axis_index("ctx")] = own_ref[...]
+    block_right(0, 0).start()
+    block_left(0, 0).start()
+
+    def middle(s, carry):
+        block_right(s, s - 1).wait_recv()
+        block_right(s, s).start()
+        block_left(s, s - 1).wait_recv()
+        block_left(s, s).start()
+        return carry
+
+    lax.fori_loop(1, hops_left, middle, 0)
+    block_right(hops_left, hops_left - 1).wait_recv()
+    block_right(hops_left, hops_left).start()
+    block_left(hops_left, hops_left - 1).wait_recv()
+    block_right(hops_right, hops_right - 1).wait_recv()
+
+    def drain_left(s, carry):
+        block_left(s, s).wait_send()
+        return carry
+
+    def drain_right(s, carry):
+        block_right(s, s).wait_send()
+        return carry
+
+    lax.fori_loop(0, hops_left, drain_left, 0)
+    lax.fori_loop(0, hops_right, drain_right, 0)
+
+
+def sum_kernel(
+    count,
+    grad_ref,
+    proj_ref,
+    sum_ref,
+    out_right,
+    out_left,
+    in_right,
+    in_left,
+    r_send,
+    r_recv,
+    l_send,
+    l_recv,
+):
+    hops_right = count // 2
+    hops_left = count - 1 - hops_right
+    group = proj_ref.shape[0]
+    place, right, left = neighbours(count)
+
+    def sum_right(s):
+        return remote(out_right.at[s], in_right.at[s], (r_send, r_recv), s, right)
+
+    def sum_left(s):
+        return remote(out_left.at[s], in_left.at[s], (l_send, l_recv), s, left)
+
+    def term(offset):
+        owner = place(offset)
+        return jnp.dot(
+            grad_ref[owner // group], proj_ref[lax.rem(owner, group)], preferred_element_type=F32
+        )
+
+    def step(s, first, both):
+        own = term(hops_right - s)
+        if not first:
+            sum_right(s - 1).wait_recv()
+            own = own + in_right[s - 1].astype(F32)
+        out_right[s] = own.astype(BF16)
+        sum_right(s).start()
+        if both:
+            own = term(s - hops_left)
+            if not first:
+                sum_left(s - 1).wait_recv()
+                own = own + in_left[s - 1].astype(F32)
+            out_left[s] = own.astype(BF16)
+            sum_left(s).start()
+
+    def middle(s, carry):
+        step(s, False, True)
+        return carry
+
+    step(0, True, True)
+    lax.fori_loop(1, hops_left, middle, 0)
+    step(hops_left, False, False)
+
+    own = term(0)
+    sum_left(hops_left - 1).wait_recv()
+    own = own + in_left[hops_left - 1].astype(F32)
+    sum_right(hops_right - 1).wait_recv()
+    own = own + in_right[hops_right - 1].astype(F32)
+    sum_ref[...] = own.astype(BF16)
+
+    def drain_left(s, carry):
+        sum_left(s).wait_send()
+        return carry
+
+    def drain_right(s, carry):
+        sum_right(s).wait_send()
+        return carry
+
+    lax.fori_loop(0, hops_left, drain_left, 0)
+    lax.fori_loop(0, hops_right, drain_right, 0)
+
+
+def ring_call(kernel, number, operands, result, scratch, count, flops):
+    right = count // 2
+    left = count - 1 - right
+    dma = pltpu.SemaphoreType.DMA
+    vmem = pl.BlockSpec(memory_space=pltpu.VMEM)
+    return pl.pallas_call(
+        functools.partial(kernel, count),
+        out_shape=jax.ShapeDtypeStruct(result, BF16),
+        in_specs=[vmem] * len(operands),
+        out_specs=vmem,
+        scratch_shapes=scratch + [dma((right,)), dma((right,)), dma((left,)), dma((left,))],
+        compiler_params=pltpu.CompilerParams(
+            collective_id=number, has_side_effects=True, vmem_limit_bytes=48 << 20
+        ),
+        cost_estimate=pl.CostEstimate(
+            flops=flops, bytes_accessed=64 << 20, transcendentals=0
+        ),
+    )(*operands)
+
+
+def ring_gather(block, count):
+    return ring_call(gather_kernel, 0, (block,), (count,) + block.shape, [], count, 0)
+
+
+def ring_sum(grad_groups, proj_heads, count):
+    rows, depth = grad_groups.shape[1:]
+    width = proj_heads.shape[2]
+    right = count // 2
+    left = count - 1 - right
+    scratch = [pltpu.VMEM((hops, rows, width), BF16) for hops in (right, left, right, left)]
+    flops = 2 * count * rows * depth * width
+    return ring_call(
+        sum_kernel, 1, (grad_groups, proj_heads), (rows, width), scratch, count, flops
+    )
 
 
 def shards(queries, rotated_keys, value_vectors, out_grad, out_proj, seg_ids):
@@ -52,10 +251,6 @@
     own_kv = mine[:, q_width:]
     received = [shifted(own_kv, "ctx", group * (d + 1)) for d in range(halo_blocks)]
     kv = jnp.concatenate(received[::-1] + [own_kv], axis=0)
-    keys, values = kv[:, :head_size], kv[:, head_size:]
-
-    proj_full = lax.all_gather(out_proj, "ctx", axis=0, tiled=True)
-
     columns = out_grad.shape[1]
     grad_full = jnp.zeros((tok_rows, columns * head_count), BF16)
     grad_full = lax.dynamic_update_slice_in_dim(grad_full, out_grad, head_index * columns, 1)
@@ -63,6 +258,8 @@
         block = rotated(out_grad, "head", d)
         source = lax.rem(head_index + head_count - d, head_count)
         grad_full = lax.dynamic_update_slice_in_dim(grad_full, block, source * columns, 1)
+    grad_full, kv = lax.optimization_barrier((grad_full, kv))
+    keys, values = kv[:, :head_size], kv[:, head_size:]
     grad_columns = lax.all_to_all(grad_full, "ctx", 1, 0, tiled=True)
 
     first_row = (ctx_index // group) * rows
@@ -83,23 +280,31 @@
     probs = weights / jnp.sum(weights, axis=2, keepdims=True)
     probs_bf = probs.astype(BF16)
     attended = jnp.einsum("hts,sd->htd", probs_bf, values, preferred_element_type=F32).astype(BF16)
-    attended_tok = to_tokens(attended.transpose(1, 0, 2).reshape(rows, q_width))
-    attended_all = lax.all_gather(attended_tok, "ctx", axis=0, tiled=True)
-
-    grad_att_tok = matmul(grad_full, proj_full, ((1,), (0,))).astype(BF16)
-    grad_att = to_heads(grad_att_tok).reshape(rows, per_kv, head_size).transpose(1, 0, 2)
-
-    def out_columns(which):
-        block = lax.dynamic_slice_in_dim(proj_full, which * columns, columns, 0)
-        return matmul(attended_tok, block, ((1,), (1,)))
-
-    layer_out = out_columns(head_index)
+
+    attended_all = ring_gather(attended.transpose(1, 0, 2).reshape(rows, q_width), ctx_count)
+    attended_all = attended_all.reshape(ctx_count // group, group, rows, q_width)
+    attended_all = attended_all.transpose(0, 2, 1, 3).reshape(ctx_count * tok_rows, group * q_width)
+    out_part = matmul(attended_all, out_proj, ((1,), (1,))).astype(BF16)
+    out_part, grad_columns = lax.optimization_barrier((out_part, grad_columns))
+    out_part = lax.all_to_all(out_part, "ctx", 0, 1, tiled=True)
+    layer_out = lax.dynamic_slice_in_dim(out_part, head_index * columns, columns, 1).astype(F32)
     for d in range(1, head_count):
         target = lax.rem(head_index + d, head_count)
-        layer_out = layer_out + rotated(out_columns(target).astype(BF16), "head", d).astype(F32)
+        block = lax.dynamic_slice_in_dim(out_part, target * columns, columns, 1)
+        layer_out = layer_out + rotated(block, "head", d).astype(F32)
     layer_out = layer_out.astype(BF16)
 
     grad_proj = matmul(grad_columns, attended_all, ((0,), (0,))) * (ctx_count * tok_rows) ** (-0.5)
+
+    proj_rows = out_proj.shape[0]
+    pad = -proj_rows % 128
+    proj_heads = out_proj.reshape(proj_rows, group, q_width).transpose(1, 0, 2)
+    grad_att = ring_sum(
+        jnp.pad(grad_columns.reshape(-1, rows, proj_rows), ((0, 0), (0, 0), (0, pad))),
+        jnp.pad(proj_heads, ((0, 0), (0, pad), (0, 0))),
+        ctx_count,
+    )
+    grad_att = grad_att.reshape(rows, per_kv, head_size).transpose(1, 0, 2)
 
     grad_probs = jnp.einsum("htd,sd->hts", grad_att, values, preferred_element_type=F32)
     row_delta = jnp.sum(grad_att.astype(F32) * attended.astype(F32), axis=2, keepdims=True)

time: 250 us -> 241 us (0.964)
  Pallas kernels: 0 us -> 78.2 us
  waiting for transfers between devices: 120 us -> 61.4 us
  blocking collectives: 26.3 us -> 0 us
  between operations: 14.3 us -> 1.05 us
  matrix products: 36.3 us -> 23.9 us
  local copies, waits for them, and re-layouts: 15.8 us -> 26.7 us
  starting transfers between devices: 27.2 us -> 37.5 us
  other arithmetic: 6 us -> 11 us
    pallas_call x0 -> x2, Pallas kernels: none -> 78.2 us  [ring_call(): pl.pallas_call(functools.partial(kernel, count), out_shape=jax.ShapeDtype...]
    all_gather x2 -> x0, waiting for transfers between devices: 56.4 us -> none  [the longest x1 56.4 us: shards(): proj_full = lax.all_gather(out_proj, 'ctx', axis=0, tiled=True)]
    all_to_all x2 -> x0, blocking collectives: 26.3 us -> none  [to_tokens(): lax.all_to_all(value, 'ctx', 0, 1, axis_index_groups=groups, tiled=True)]
    dot_general x4 -> x2, matrix products: 21.7 us -> 7.56 us  [matmul(): return lax.dot_general(a, b, (dims, ((), ())), preferred_element_type=F32)]
    all_to_all x0 -> x2, starting transfers between devices: none -> 7.67 us  [the longest x1 4.2 us: shards(): out_part = lax.all_to_all(out_part, 'ctx', 0, 1, tiled=True)]
    all_to_all x1, starting transfers between devices: 3.7 us -> 10.4 us  [shards(): grad_columns = lax.all_to_all(grad_full, 'ctx', 1, 0, tiled=True)]
    ppermute x2, waiting for transfers between devices: 13.6 us -> 7.42 us  [rotated(): lax.ppermute(value, axis, [(i, (i + by) % count) for i in range(count)])]
    ppermute x4, waiting for transfers between devices: 41 us -> 46.5 us  [shifted(): return lax.ppermute(value, axis, pairs)]
  transfers between devices with their start and end apart: 11 -> 10, of which waited for: 8 -> 7; matrix products, arithmetic and copies ran while one was open for 15% -> 18% of each run, Pallas kernels for 0% -> 19%
where the time goes in v3:
time: 241 us; the launch traced here: 240 us
  Pallas kernels  78.2 us (32%)
  waiting for transfers between devices  61.4 us (25%)
  starting transfers between devices  37.5 us (16%)
  local copies, waits for them, and re-layouts  26.7 us (11%)
  matrix products  23.9 us (10%)
  other arithmetic  11 us (5%)
    pallas_call x2, Pallas kernels, ring_call(): pl.pallas_call(functools.partial(kernel, count), out_shape=jax.ShapeDtype...  78.2 us
    ppermute x4, waiting for transfers between devices, shifted(): return lax.ppermute(value, axis, pairs)  46.5 us
    ppermute x4, starting transfers between devices, shifted(): return lax.ppermute(value, axis, pairs)  11.5 us
    all_to_all x1, starting transfers between devices, shards(): grad_columns = lax.all_to_all(grad_full, 'ctx', 1, 0, tiled=True)  10.4 us
    unnamed x33, local copies, waits for them, and re-layouts  9.57 us
    dot_general x2, matrix products, matmul(): return lax.dot_general(a, b, (dims, ((), ())), preferred_element_type=F32)  7.56 us
    ppermute x2, waiting for transfers between devices, rotated(): lax.ppermute(value, axis, [(i, (i + by) % count) for i in range(count)])  7.42 us
    sub x1, matrix products, shards(): weights = jnp.where(allowed, jnp.exp(scores - top_score), 0.0)  7.14 us
  transfers between devices with their start and end apart: 10, of which 7 were waited for; matrix products, arithmetic and copies ran while one was open for 18% of the time, Pallas kernels for 19%

profile of v3, /device:TPU:0, one launch (start us, length us, event | category | flops | bytes accessed | tf_op | source)
XLA Modules:
  0.0 239.8 jit_solution(9014696972048557325)
XLA Ops:
  0.7 1.2 reshape.73
  1.9 0.9 copy.85
  2.9 0.9 copy.86
  3.8 0.8 pad_maximum_fusion.2
  4.6 4.2 %all-to-all-start = ((bf16[128,4,512]{2,0,1:T(8,128)(2,1)}), bf16[128,4,512]{2,0,1:T(8,128)(2,1)S(1)}, u32[]{:S(2)}, u32[]{:S(2)}) async-start(bf16[128,4,512]{2,0,1:T(8,128)(2,1)} %pad_maximum_fusion.2), calls=%async_computation | async-start | bytes 1048576 | tf_op jit(solution)/shard_map/all_to_all | solution.py:241
  9.2 2.3 collective-permute-start
  11.8 5.9 %all-to-all-done = bf16[128,4,512]{2,0,1:T(8,128)(2,1)S(1)} async-done(((bf16[128,4,512]{2,0,1:T(8,128)(2,1)}), bf16[128,4,512]{2,0,1:T(8,128)(2,1)S(1)}, u32[]{:S(2)}, u32[]{:S(2)}) %all-to-all-start) | async-done | bytes 524320 | tf_op jit(solution)/shard_map/all_to_all | solution.py:241
  17.8 5.2 %collective-permute-start.1 = (bf16[512,256]{1,0:T(8,128)(2,1)S(1)}, bf16[512,256]{1,0:T(8,128)(2,1)S(1)}, u32[]{:S(2)}, u32[]{:S(2)}) collective-permute-start(bf16[512,256]{1,0:T(8,128)(2,1)S(1)} %get-tuple-element.38), channel_id=1, source_target_pairs={{0,16},{2,18},{4,20},{6,22},{8,24},{10,26},{12,28},{14,30},{1,17},... | collective-permute-start | bytes 786440 | tf_op jit(solution)/shard_map/ppermute | solution.py:18
  22.9 3.5 %collective-permute-start.2 = (bf16[512,256]{1,0:T(8,128)(2,1)S(1)}, bf16[512,256]{1,0:T(8,128)(2,1)S(1)}, u32[]{:S(2)}, u32[]{:S(2)}) collective-permute-start(bf16[512,256]{1,0:T(8,128)(2,1)S(1)} %get-tuple-element.38), channel_id=1, source_target_pairs={{0,8},{2,10},{4,12},{6,14},{8,16},{10,18},{12,20},{14,22},{16,24},... | collective-permute-start | bytes 786440 | tf_op jit(solution)/shard_map/ppermute | solution.py:18
  26.4 1.3 broadcast_in_dim.15
  27.7 0.9 constant_dynamic-update-slice_fusion.1
  28.6 1.1 collective-permute-done.1
  29.7 4.4 %collective-permute-done.2 = bf16[512,256]{1,0:T(8,128)(2,1)S(1)} collective-permute-done((bf16[512,256]{1,0:T(8,128)(2,1)S(1)}, bf16[512,256]{1,0:T(8,128)(2,1)S(1)}, u32[]{:S(2)}, u32[]{:S(2)}) %collective-permute-start.2) | collective-permute-done | bytes 262176 | tf_op jit(solution)/shard_map/ppermute | solution.py:18
  34.1 2.3 constant_dynamic-update-slice_fusion
  36.4 10.4 %all-to-all-start.1 = ((bf16[128,16,336]{0,2,1:T(8,128)(2,1)}), bf16[128,16,336]{0,2,1:T(8,128)(2,1)S(1)}, u32[]{:S(2)}, u32[]{:S(2)}) async-start(bf16[128,16,336]{0,2,1:T(8,128)(2,1)} %bitcast.12), calls=%async_computation.1 | async-start | bytes 2752512 | tf_op jit(solution)/shard_map/all_to_all | solution.py:263
  46.9 2.1 fusion.6
  48.9 7.1 %fusion.42 = (f32[2,512]{1,0:T(2,128)S(1)}, f32[2,512,1536]{2,1,0:T(8,128)}) fusion(pred[512,1536]{1,0:T(8,128)(4,1)} %fusion.6, bf16[1536,256]{1,0:T(8,128)(2,1)S(1)} %pad_maximum_fusion.1, bf16[64,2,8,128]{3,2,1,0:T(8,128)(2,1)S(1)} %get-tuple-element.37), kind=kOutput, calls=%fused_computation.67 | convolution fusion | flops 410519040 | bytes 8523776 | tf_op jit(solution)/shard_map/sub | solution.py:279
  56.1 3.6 %fusion.8 = bf16[2,512,1536]{2,1,0:T(8,128)(2,1)S(1)} fusion(f32[2,512,1536]{2,1,0:T(8,128)} %get-tuple-element.40, f32[2,512]{1,0:T(2,128)S(1)} %get-tuple-element.39), kind=kLoop, calls=%fused_computation.14 | loop fusion | flops 3145728 | bytes 9441280 | tf_op jit(solution)/shard_map/convert_element_type | solution.py:281
  59.7 1.2 convolution_convert_fusion.1
  61.6 44.9 %shard_map.101 = bf16[16,512,256]{2,1,0:T(8,128)(2,1)S(1)} custom-call(bf16[512,256]{1,0:T(8,128)(2,1)S(1)} %copy.113.own_ref), custom_call_target="tpu_custom_call" | custom-call | bytes 67108864 | tf_op jit(solution)/shard_map/pallas_call | solution.py:194
  106.5 3.2 %copy.92 = bf16[4,4,512,256]{3,1,2,0:T(4,128)(2,1)S(1)} copy(bf16[4,4,512,256]{3,2,1,0:T(8,128)(2,1)S(1)} %bitcast.102) | data formatting | bytes 8388608 | tf_op jit(solution)/shard_map/reshape | solution.py:285
  109.7 1.0 copy.123
  110.8 2.0 copy-done.2
  112.8 2.7 %convolution_convert_fusion = bf16[2048,336]{0,1:T(8,128)(2,1)} fusion(bf16[2048,1024]{1,0:T(8,128)(2,1)S(1)} %bitcast.107, bf16[336,1024]{1,0:T(8,128)(2,1)S(1)} %copy-done.10), kind=kOutput, calls=%fused_computation.13 | convolution fusion | flops 1409974272 | bytes 6258688 | tf_op jit(solution)/shard_map/dot_general | solution.py:27
  115.6 1.3 copy_bitcast_fusion
  116.8 1.8 copy.95
  118.8 33.3 %shard_map.102 = bf16[512,256]{1,0:T(8,128)(2,1)S(1)} custom-call(bf16[4,512,384]{2,1,0:T(8,128)(2,1)S(1)} %pad.9.grad_ref, bf16[4,384,256]{2,1,0:T(8,128)(2,1)S(1)} %pad.10.proj_ref), custom_call_target="tpu_custom_call" | custom-call | flops 1610612736 | bytes 67108864 | tf_op jit(solution)/shard_map/pallas_call | solution.py:194
  152.4 2.6 %convolution_bitcast_fusion = f32[1536,128]{0,1:T(8,128)S(1)} fusion(bf16[2,512,128]{1,2,0:T(8,128)(2,1)S(1)} %bitcast.110, bf16[2,512,1536]{2,1,0:T(8,128)(2,1)} %copy-done), kind=kOutput, calls=%fused_computation.15 | convolution fusion | flops 402653184 | bytes 4194304 | tf_op jit(solution)/shard_map/hts,htd->sd/dot_general | solution.py:313
  155.0 1.3 copy_bitcast_fusion.1
  156.3 4.2 %all-to-all-start.2 = ((bf16[16,128,336]{1,2,0:T(8,128)(2,1)}), bf16[16,128,336]{1,2,0:T(8,128)(2,1)S(1)}, u32[]{:S(2)}, u32[]{:S(2)}) async-start(bf16[16,128,336]{1,2,0:T(8,128)(2,1)} %copy_bitcast_fusion.1), calls=%async_computation.2 | async-start | bytes 2752512 | tf_op jit(solution)/shard_map/all_to_all | solution.py:289
  160.6 3.6 %multiply_convert_fusion = bf16[2,512,1536]{2,1,0:T(8,128)(2,1)S(1)} fusion(bf16[2,512,128]{1,2,0:T(8,128)(2,1)S(1)} %bitcast.111, f32[2,512]{1,0:T(2,128)S(1)} %multiply_reduce_fusion, f32[2,512,1536]{2,1,0:T(8,128)} %get-tuple-element.40, f32[2,512]{1,0:T(2,128)S(1)} %get-tuple-element.39, bf16[1536,256]{1,0:T(8,128)(2,1)S(1)} %pad_maximum_fusion.1), kind=kOutput, calls=%fused_computation.1 | convolution fusion | flops 408944640 | bytes 10100736 | tf_op jit(solution)/shard_map/htd,sd->hts/dot_general | solution.py:309
  165.8 1.3 collective-permute-start.4
  167.1 1.5 collective-permute-start.5
  168.6 1.2 fusion.12
  170.1 21.4 %collective-permute-done.4 = bf16[512,256]{0,1:T(8,128)(2,1)} collective-permute-done((bf16[512,256]{0,1:T(8,128)(2,1)}, bf16[512,256]{0,1:T(8,128)(2,1)}, u32[]{:S(2)}, u32[]{:S(2)}) %collective-permute-start.4) | collective-permute-done | bytes 262176 | tf_op jit(solution)/shard_map/ppermute | solution.py:18
  191.5 19.6 %collective-permute-done.5 = bf16[512,256]{0,1:T(8,128)(2,1)} collective-permute-done((bf16[512,256]{0,1:T(8,128)(2,1)}, bf16[512,256]{0,1:T(8,128)(2,1)}, u32[]{:S(2)}, u32[]{:S(2)}) %collective-permute-start.5) | collective-permute-done | bytes 262176 | tf_op jit(solution)/shard_map/ppermute | solution.py:18
  211.1 1.1 fusion.18
  212.2 0.8 copy.118
  213.1 1.8 pad_maximum_fusion.3
  214.9 3.5 %all-to-all-start.3 = ((bf16[4,128,512]{2,1,0:T(8,128)(2,1)}), bf16[4,128,512]{2,1,0:T(8,128)(2,1)S(1)}, u32[]{:S(2)}, u32[]{:S(2)}) async-start(bf16[4,128,512]{2,1,0:T(8,128)(2,1)} %pad_maximum_fusion.3), calls=%async_computation.3 | async-start | bytes 1048576 | tf_op jit(solution)/shard_map/all_to_all | solution.py:244
  218.3 0.9 constant_dynamic-slice_fusion
  219.2 1.5 collective-permute-start.3
  220.7 4.9 %convolution_multiply_fusion = f32[336,1024]{1,0:T(8,128)} fusion(bf16[2048,336]{0,1:T(8,128)(2,1)S(1)} %copy-done.1, bf16[2048,1024]{1,0:T(8,128)(2,1)} %bitcast.108), kind=kOutput, calls=%fused_computation.22 | convolution fusion | flops 1409630208 | bytes 6946816 | tf_op jit(solution)/shard_map/dot_general | solution.py:27
  225.6 1.6 all-to-all-done.3
  227.5 0.9 copy.105
  229.9 7.4 %collective-permute-done.3 = bf16[128,2688]{0,1:T(8,128)(2,1)} collective-permute-done((bf16[128,2688]{0,1:T(8,128)(2,1)}, bf16[128,2688]{0,1:T(8,128)(2,1)}, u32[]{:S(2)}, u32[]{:S(2)}) %collective-permute-start.3) | collective-permute-done | bytes 688160 | tf_op jit(solution)/shard_map/ppermute | solution.py:23
  237.4 1.3 add_convert_fusion
  238.6 1.1 copy.104
  (50 shorter events, 5.6 us)
Async XLA Ops:
  0.6 8.2 %copy-start.8 = (bf16[128,2688]{1,0:T(8,128)(2,1)S(1)}, bf16[128,2688]{1,0:T(8,128)(2,1)}, u32[]{:S(2)}) copy-start(bf16[128,2688]{1,0:T(8,128)(2,1)} %param.9) | copy-start | bytes 2064388
  0.6 10.8 %copy-start.9 = (bf16[336,1024]{1,0:T(8,128)(2,1)S(1)}, bf16[336,1024]{1,0:T(8,128)(2,1)}, u32[]{:S(2)}) copy-start(bf16[336,1024]{1,0:T(8,128)(2,1)} %param.10) | copy-start | bytes 2064388
  0.7 10.9 %copy-start.11 = (s32[2048]{0:T(1024)S(1)}, s32[2048]{0:T(1024)}, u32[]{:S(2)}) copy-start(s32[2048]{0:T(1024)} %param.11) | copy-start | bytes 24580
  4.6 13.1 %all-to-all-start = ((bf16[128,4,512]{2,0,1:T(8,128)(2,1)}), bf16[128,4,512]{2,0,1:T(8,128)(2,1)S(1)}, u32[]{:S(2)}, u32[]{:S(2)}) async-start(bf16[128,4,512]{2,0,1:T(8,128)(2,1)} %pad_maximum_fusion.2), calls=%async_computation | async-start | bytes 1048576 | tf_op jit(solution)/shard_map/all_to_all | solution.py:241
  9.2 24.9 %collective-permute-start = (bf16[128,2688]{0,1:T(8,128)(2,1)S(1)}, bf16[128,2688]{0,1:T(8,128)(2,1)}, u32[]{:S(2)}, u32[]{:S(2)}) collective-permute-start(bf16[128,2688]{0,1:T(8,128)(2,1)S(1)} %copy.88), channel_id=1, source_target_pairs={{0,1},{1,0},{2,3},{3,2},{4,5},{5,4},{6,7},{7,6},{8,9},{9,8},{10,11... | collective-permute-start | bytes 2064392 | tf_op jit(solution)/shard_map/ppermute | solution.py:23
  17.8 31.2 %copy-start.6 = (bf16[64,2,8,128]{3,2,1,0:T(8,128)(2,1)}, bf16[64,2,8,128]{3,2,1,0:T(8,128)(2,1)S(1)}, u32[]{:S(2)}) copy-start(bf16[64,2,8,128]{3,2,1,0:T(8,128)(2,1)S(1)} %get-tuple-element.37) | copy-start | bytes 786436
  17.8 11.9 %collective-permute-start.1 = (bf16[512,256]{1,0:T(8,128)(2,1)S(1)}, bf16[512,256]{1,0:T(8,128)(2,1)S(1)}, u32[]{:S(2)}, u32[]{:S(2)}) collective-permute-start(bf16[512,256]{1,0:T(8,128)(2,1)S(1)} %get-tuple-element.38), channel_id=1, source_target_pairs={{0,16},{2,18},{4,20},{6,22},{8,24},{10,26},{12,28},{14,30},{1,17},... | collective-permute-start | bytes 786440 | tf_op jit(solution)/shard_map/ppermute | solution.py:18
  22.9 11.1 %collective-permute-start.2 = (bf16[512,256]{1,0:T(8,128)(2,1)S(1)}, bf16[512,256]{1,0:T(8,128)(2,1)S(1)}, u32[]{:S(2)}, u32[]{:S(2)}) collective-permute-start(bf16[512,256]{1,0:T(8,128)(2,1)S(1)} %get-tuple-element.38), channel_id=1, source_target_pairs={{0,8},{2,10},{4,12},{6,14},{8,16},{10,18},{12,20},{14,22},{16,24},... | collective-permute-start | bytes 786440 | tf_op jit(solution)/shard_map/ppermute | solution.py:18
  34.1 126.5 %copy-start.3 = (bf16[1536,256]{1,0:T(8,128)(2,1)}, bf16[1536,256]{1,0:T(8,128)(2,1)S(1)}, u32[]{:S(2)}) copy-start(bf16[1536,256]{1,0:T(8,128)(2,1)S(1)} %pad_maximum_fusion.1) | copy-start | bytes 2359300
  36.4 79.1 %all-to-all-start.1 = ((bf16[128,16,336]{0,2,1:T(8,128)(2,1)}), bf16[128,16,336]{0,2,1:T(8,128)(2,1)S(1)}, u32[]{:S(2)}, u32[]{:S(2)}) async-start(bf16[128,16,336]{0,2,1:T(8,128)(2,1)} %bitcast.12), calls=%async_computation.1 | async-start | bytes 2752512 | tf_op jit(solution)/shard_map/all_to_all | solution.py:263
  59.7 1.8 copy-start
  109.7 3.1 %copy-start.10 = (bf16[336,1024]{1,0:T(8,128)(2,1)S(1)}, bf16[336,1024]{1,0:T(8,128)(2,1)}, u32[]{:S(2)}) copy-start(bf16[336,1024]{1,0:T(8,128)(2,1)} %param.10) | copy-start | bytes 2064388
  110.8 2.1 copy-start.2
  152.4 2.6 %copy-start.5 = (bf16[2048,336]{0,1:T(8,128)(2,1)S(1)}, bf16[2048,336]{0,1:T(8,128)(2,1)}, u32[]{:S(2)}) copy-start(bf16[2048,336]{0,1:T(8,128)(2,1)} %convolution_convert_fusion) | copy-start | bytes 4128772
  156.3 58.6 %all-to-all-start.2 = ((bf16[16,128,336]{1,2,0:T(8,128)(2,1)}), bf16[16,128,336]{1,2,0:T(8,128)(2,1)S(1)}, u32[]{:S(2)}, u32[]{:S(2)}) async-start(bf16[16,128,336]{1,2,0:T(8,128)(2,1)} %copy_bitcast_fusion.1), calls=%async_computation.2 | async-start | bytes 2752512 | tf_op jit(solution)/shard_map/all_to_all | solution.py:289
  160.6 3.6 %copy-start.7 = (bf16[64,2,8,128]{3,2,1,0:T(8,128)(2,1)S(1)}, bf16[64,2,8,128]{3,2,1,0:T(8,128)(2,1)}, u32[]{:S(2)}) copy-start(bf16[64,2,8,128]{3,2,1,0:T(8,128)(2,1)} %copy-done.6) | copy-start | bytes 786436
  164.2 4.4 %copy-start.4 = (bf16[1536,256]{1,0:T(8,128)(2,1)S(1)}, bf16[1536,256]{1,0:T(8,128)(2,1)}, u32[]{:S(2)}) copy-start(bf16[1536,256]{1,0:T(8,128)(2,1)} %copy-done.3) | copy-start | bytes 2359300
  165.8 25.7 %collective-permute-start.4 = (bf16[512,256]{0,1:T(8,128)(2,1)}, bf16[512,256]{0,1:T(8,128)(2,1)}, u32[]{:S(2)}, u32[]{:S(2)}) collective-permute-start(bf16[512,256]{0,1:T(8,128)(2,1)} %get-tuple-element.33), channel_id=1, source_target_pairs={{8,0},{10,2},{12,4},{14,6},{16,8},{18,10},{20,12},{22,14},{24,16},... | collective-permute-start | bytes 786440 | tf_op jit(solution)/shard_map/ppermute | solution.py:18
  167.1 44.0 %collective-permute-start.5 = (bf16[512,256]{0,1:T(8,128)(2,1)}, bf16[512,256]{0,1:T(8,128)(2,1)}, u32[]{:S(2)}, u32[]{:S(2)}) collective-permute-start(bf16[512,256]{0,1:T(8,128)(2,1)} %get-tuple-element.34), channel_id=1, source_target_pairs={{16,0},{18,2},{20,4},{22,6},{24,8},{26,10},{28,12},{30,14},{17,1},... | collective-permute-start | bytes 786440 | tf_op jit(solution)/shard_map/ppermute | solution.py:18
  212.2 8.5 %copy-start.1 = (bf16[2048,336]{0,1:T(8,128)(2,1)S(1)}, bf16[2048,336]{0,1:T(8,128)(2,1)}, u32[]{:S(2)}) copy-start(bf16[2048,336]{0,1:T(8,128)(2,1)} %copy_bitcast_fusion) | copy-start | bytes 4128772
  214.9 12.3 %all-to-all-start.3 = ((bf16[4,128,512]{2,1,0:T(8,128)(2,1)}), bf16[4,128,512]{2,1,0:T(8,128)(2,1)S(1)}, u32[]{:S(2)}, u32[]{:S(2)}) async-start(bf16[4,128,512]{2,1,0:T(8,128)(2,1)} %pad_maximum_fusion.3), calls=%async_computation.3 | async-start | bytes 1048576 | tf_op jit(solution)/shard_map/all_to_all | solution.py:244
  219.2 18.1 %collective-permute-start.3 = (bf16[128,2688]{0,1:T(8,128)(2,1)}, bf16[128,2688]{0,1:T(8,128)(2,1)}, u32[]{:S(2)}, u32[]{:S(2)}) collective-permute-start(bf16[128,2688]{0,1:T(8,128)(2,1)} %constant_dynamic-slice_fusion), channel_id=1, source_target_pairs={{0,1},{1,0},{2,3},{3,2},{4,5},{5,4},{6,7},{7,6},{8,9},{9,8},{10,11... | collective-permute-start | bytes 2064392 | tf_op jit(solution)/shard_map/ppermute | solution.py:23

commit v4 on v3

--- a/solution.py
+++ b/solution.py
@@ -43,7 +43,8 @@
     return down * half + pair * 2 + core
 
 
-def neighbours(count):
+def neighbours(count, everyone=False):
+    me = lax.axis_index("ctx")
     here = ring_position(lax.axis_index("ctx"), count)
 
     def place(offset):
@@ -51,11 +52,12 @@
 
     right, left = {"ctx": place(1)}, {"ctx": place(-1)}
     barrier = pltpu.get_barrier_semaphore()
-    for neighbour in (left, right):
-        pl.semaphore_signal(
-            barrier, inc=1, device_id=neighbour, device_id_type=pl.DeviceIdType.MESH
-        )
-    pl.semaphore_wait(barrier, 2)
+    others = (left, right)
+    if everyone:
+        others = [{"ctx": lax.rem(me + d, count)} for d in range(1, count)]
+    for other in others:
+        pl.semaphore_signal(barrier, inc=1, device_id=other, device_id_type=pl.DeviceIdType.MESH)
+    pl.semaphore_wait(barrier, len(others))
     return place, right, left
 
 
@@ -117,20 +119,39 @@
     count,
     grad_ref,
     proj_ref,
+    part_ref,
     sum_ref,
+    blocks_ref,
     out_right,
     out_left,
     in_right,
     in_left,
+    b_send,
+    b_recv,
     r_send,
     r_recv,
     l_send,
     l_recv,
 ):
+    me = lax.axis_index("ctx")
     hops_right = count // 2
     hops_left = count - 1 - hops_right
     group = proj_ref.shape[0]
-    place, right, left = neighbours(count)
+    place, right, left = neighbours(count, everyone=True)
+
+    def block_out(d):
+        target = lax.rem(me + d, count)
+        return remote(
+            part_ref.at[target], blocks_ref.at[me], (b_send, b_recv), d - 1, {"ctx": target}
+        )
+
+    def block_in(d):
+        source = lax.rem(me - d + count, count)
+        return remote(
+            part_ref.at[source], blocks_ref.at[source], (b_send, b_recv), d - 1, {"ctx": source}
+        )
+
+    blocks_ref[me] = part_ref[me]
 
     def sum_right(s):
         return remote(out_right.at[s], in_right.at[s], (r_send, r_recv), s, right)
@@ -151,6 +172,7 @@
             own = own + in_right[s - 1].astype(F32)
         out_right[s] = own.astype(BF16)
         sum_right(s).start()
+        block_out(2 * s + 1).start()
         if both:
             own = term(s - hops_left)
             if not first:
@@ -158,6 +180,7 @@
                 own = own + in_left[s - 1].astype(F32)
             out_left[s] = own.astype(BF16)
             sum_left(s).start()
+            block_out(2 * s + 2).start()
 
     def middle(s, carry):
         step(s, False, True)
@@ -174,6 +197,13 @@
     own = own + in_right[hops_right - 1].astype(F32)
     sum_ref[...] = own.astype(BF16)
 
+    def take_blocks(d, carry):
+        block_in(d).wait_recv()
+        block_out(d).wait_send()
+        return carry
+
+    lax.fori_loop(1, count, take_blocks, 0)
+
     def drain_left(s, carry):
         sum_left(s).wait_send()
         return carry
@@ -186,16 +216,16 @@
     lax.fori_loop(0, hops_right, drain_right, 0)
 
 
-def ring_call(kernel, number, operands, result, scratch, count, flops):
+def ring_call(kernel, number, operands, results, scratch, count, flops):
     right = count // 2
     left = count - 1 - right
     dma = pltpu.SemaphoreType.DMA
     vmem = pl.BlockSpec(memory_space=pltpu.VMEM)
     return pl.pallas_call(
         functools.partial(kernel, count),
-        out_shape=jax.ShapeDtypeStruct(result, BF16),
+        out_shape=[jax.ShapeDtypeStruct(shape, BF16) for shape in results],
         in_specs=[vmem] * len(operands),
-        out_specs=vmem,
+        out_specs=[vmem] * len(results),
         scratch_shapes=scratch + [dma((right,)), dma((right,)), dma((left,)), dma((left,))],
         compiler_params=pltpu.CompilerParams(
             collective_id=number, has_side_effects=True, vmem_limit_bytes=48 << 20
@@ -207,18 +237,25 @@
 
 
 def ring_gather(block, count):
-    return ring_call(gather_kernel, 0, (block,), (count,) + block.shape, [], count, 0)
-
-
-def ring_sum(grad_groups, proj_heads, count):
+    return ring_call(gather_kernel, 0, (block,), [(count,) + block.shape], [], count, 0)[0]
+
+
+def ring_sum(grad_groups, proj_heads, parts, count):
     rows, depth = grad_groups.shape[1:]
     width = proj_heads.shape[2]
     right = count // 2
     left = count - 1 - right
     scratch = [pltpu.VMEM((hops, rows, width), BF16) for hops in (right, left, right, left)]
+    scratch = scratch + [pltpu.SemaphoreType.DMA((count - 1,))] * 2
     flops = 2 * count * rows * depth * width
     return ring_call(
-        sum_kernel, 1, (grad_groups, proj_heads), (rows, width), scratch, count, flops
+        sum_kernel,
+        1,
+        (grad_groups, proj_heads, parts),
+        [(rows, width), parts.shape],
+        scratch,
+        count,
+        flops,
     )
 
 
@@ -285,25 +322,24 @@
     attended_all = attended_all.reshape(ctx_count // group, group, rows, q_width)
     attended_all = attended_all.transpose(0, 2, 1, 3).reshape(ctx_count * tok_rows, group * q_width)
     out_part = matmul(attended_all, out_proj, ((1,), (1,))).astype(BF16)
-    out_part, grad_columns = lax.optimization_barrier((out_part, grad_columns))
-    out_part = lax.all_to_all(out_part, "ctx", 0, 1, tiled=True)
-    layer_out = lax.dynamic_slice_in_dim(out_part, head_index * columns, columns, 1).astype(F32)
-    for d in range(1, head_count):
-        target = lax.rem(head_index + d, head_count)
-        block = lax.dynamic_slice_in_dim(out_part, target * columns, columns, 1)
-        layer_out = layer_out + rotated(block, "head", d).astype(F32)
-    layer_out = layer_out.astype(BF16)
-
     grad_proj = matmul(grad_columns, attended_all, ((0,), (0,))) * (ctx_count * tok_rows) ** (-0.5)
 
     proj_rows = out_proj.shape[0]
     pad = -proj_rows % 128
     proj_heads = out_proj.reshape(proj_rows, group, q_width).transpose(1, 0, 2)
-    grad_att = ring_sum(
+    grad_att, blocks = ring_sum(
         jnp.pad(grad_columns.reshape(-1, rows, proj_rows), ((0, 0), (0, 0), (0, pad))),
         jnp.pad(proj_heads, ((0, 0), (0, pad), (0, 0))),
+        out_part.reshape(ctx_count, tok_rows, proj_rows),
         ctx_count,
     )
+    per_head = ctx_count // head_count
+    layer_out = lax.dynamic_slice_in_dim(blocks, head_index * per_head, per_head, 0).astype(F32)
+    for d in range(1, head_count):
+        target = lax.rem(head_index + d, head_count)
+        block = lax.dynamic_slice_in_dim(blocks, target * per_head, per_head, 0)
+        layer_out = layer_out + rotated(block, "head", d).astype(F32)
+    layer_out = layer_out.astype(BF16).transpose(1, 0, 2).reshape(tok_rows, columns)
     grad_att = grad_att.reshape(rows, per_kv, head_size).transpose(1, 0, 2)
 
     grad_probs = jnp.einsum("htd,sd->hts", grad_att, values, preferred_element_type=F32)

time: 241 us -> 236 us (0.979)
  waiting for transfers between devices: 61.4 us -> 33.1 us
  Pallas kernels: 78.2 us -> 102 us
  local copies, waits for them, and re-layouts: 26.7 us -> 32 us
  starting transfers between devices: 37.5 us -> 34.1 us
    pallas_call x2, Pallas kernels: 78.2 us -> 102 us  [ring_call(): pl.pallas_call(functools.partial(kernel, count), out_shape=[jax.ShapeDtyp...]
    ppermute x4, waiting for transfers between devices: 46.5 us -> 24.5 us  [shifted(): return lax.ppermute(value, axis, pairs)]
    ppermute x2, waiting for transfers between devices: 7.42 us -> 0.01 us  [rotated(): lax.ppermute(value, axis, [(i, (i + by) % count) for i in range(count)])]
    all_to_all x1 -> x0, starting transfers between devices: 4.2 us -> none  [shards(): out_part = lax.all_to_all(out_part, 'ctx', 0, 1, tiled=True)]
    unnamed x33 -> x37, local copies, waits for them, and re-layouts: 9.57 us -> 10.7 us
  transfers between devices with their start and end apart: 10 -> 9, of which waited for: 7 -> 5; matrix products, arithmetic and copies ran while one was open for 18% -> 17% of each run, Pallas kernels for 19% -> 20%
where the time goes in v4:
time: 236 us; the launch traced here: 235 us
  Pallas kernels  102 us (43%)
  starting transfers between devices  34.1 us (14%)
  waiting for transfers between devices  33.1 us (14%)
  local copies, waits for them, and re-layouts  32 us (14%)
  matrix products  22.5 us (10%)
  other arithmetic  10.1 us (4%)
    pallas_call x2, Pallas kernels, ring_call(): pl.pallas_call(functools.partial(kernel, count), out_shape=[jax.ShapeDtyp...  102 us
    ppermute x4, waiting for transfers between devices, shifted(): return lax.ppermute(value, axis, pairs)  24.5 us
    ppermute x4, starting transfers between devices, shifted(): return lax.ppermute(value, axis, pairs)  11.5 us
    unnamed x37, local copies, waits for them, and re-layouts  10.7 us
    all_to_all x1, starting transfers between devices, shards(): grad_columns = lax.all_to_all(grad_full, 'ctx', 1, 0, tiled=True)  10.5 us
    dot_general x2, matrix products, matmul(): return lax.dot_general(a, b, (dims, ((), ())), preferred_element_type=F32)  6.91 us
    sub x1, matrix products, shards(): weights = jnp.where(allowed, jnp.exp(scores - top_score), 0.0)  5.74 us
    all_to_all x1, waiting for transfers between devices, to_heads(): lax.all_to_all(value, 'ctx', 1, 0, axis_index_groups=groups, tiled=True)  5.06 us
  transfers between devices with their start and end apart: 9, of which 5 were waited for; matrix products, arithmetic and copies ran while one was open for 17% of the time, Pallas kernels for 20%

profile of v4, /device:TPU:0, one launch (start us, length us, event | category | flops | bytes accessed | tf_op | source)
XLA Modules:
  0.0 235.1 jit_solution(2407964708342086904)
XLA Ops:
  0.7 1.2 reshape.77
  1.9 0.9 copy.93
  2.9 0.9 copy.94
  4.6 4.2 %all-to-all-start = ((bf16[128,4,512]{2,0,1:T(8,128)(2,1)}), bf16[128,4,512]{2,0,1:T(8,128)(2,1)S(1)}, u32[]{:S(2)}, u32[]{:S(2)}) async-start(bf16[128,4,512]{2,0,1:T(8,128)(2,1)} %pad_maximum_fusion.2), calls=%async_computation | async-start | bytes 1048576 | tf_op jit(solution)/shard_map/all_to_all | solution.py:278
  9.2 2.3 collective-permute-start
  11.6 0.9 pad.10.proj_ref
  12.6 5.1 %all-to-all-done = bf16[128,4,512]{2,0,1:T(8,128)(2,1)S(1)} async-done(((bf16[128,4,512]{2,0,1:T(8,128)(2,1)}), bf16[128,4,512]{2,0,1:T(8,128)(2,1)S(1)}, u32[]{:S(2)}, u32[]{:S(2)}) %all-to-all-start) | async-done | bytes 524320 | tf_op jit(solution)/shard_map/all_to_all | solution.py:278
  17.8 5.2 %collective-permute-start.1 = (bf16[512,256]{1,0:T(8,128)(2,1)S(1)}, bf16[512,256]{1,0:T(8,128)(2,1)S(1)}, u32[]{:S(2)}, u32[]{:S(2)}) collective-permute-start(bf16[512,256]{1,0:T(8,128)(2,1)S(1)} %get-tuple-element.38), channel_id=1, source_target_pairs={{0,16},{2,18},{4,20},{6,22},{8,24},{10,26},{12,28},{14,30},{1,17},... | collective-permute-start | bytes 786440 | tf_op jit(solution)/shard_map/ppermute | solution.py:18
  22.9 3.5 %collective-permute-start.2 = (bf16[512,256]{1,0:T(8,128)(2,1)S(1)}, bf16[512,256]{1,0:T(8,128)(2,1)S(1)}, u32[]{:S(2)}, u32[]{:S(2)}) collective-permute-start(bf16[512,256]{1,0:T(8,128)(2,1)S(1)} %get-tuple-element.38), channel_id=1, source_target_pairs={{0,8},{2,10},{4,12},{6,14},{8,16},{10,18},{12,20},{14,22},{16,24},... | collective-permute-start | bytes 786440 | tf_op jit(solution)/shard_map/ppermute | solution.py:18
  26.4 1.3 broadcast_in_dim.14
  27.7 0.9 constant_dynamic-update-slice_fusion.1
  28.6 1.1 collective-permute-done.1
  29.7 4.4 %collective-permute-done.2 = bf16[512,256]{1,0:T(8,128)(2,1)S(1)} collective-permute-done((bf16[512,256]{1,0:T(8,128)(2,1)S(1)}, bf16[512,256]{1,0:T(8,128)(2,1)S(1)}, u32[]{:S(2)}, u32[]{:S(2)}) %collective-permute-start.2) | collective-permute-done | bytes 262176 | tf_op jit(solution)/shard_map/ppermute | solution.py:18
  34.1 2.3 constant_dynamic-update-slice_fusion
  36.4 10.5 %all-to-all-start.1 = ((bf16[128,16,336]{0,2,1:T(8,128)(2,1)}), bf16[128,16,336]{0,2,1:T(8,128)(2,1)}, u32[]{:S(2)}, u32[]{:S(2)}) async-start(bf16[128,16,336]{0,2,1:T(8,128)(2,1)} %bitcast.3), calls=%async_computation.1 | async-start | bytes 2752512 | tf_op jit(solution)/shard_map/all_to_all | solution.py:300
  46.9 1.2 fusion.6
  48.1 5.7 %fusion.45 = (f32[2,512]{1,0:T(2,128)S(1)}, f32[2,512,1536]{2,1,0:T(8,128)}) fusion(pred[512,1536]{1,0:T(8,128)(4,1)S(1)} %fusion.6, bf16[1536,256]{1,0:T(8,128)(2,1)S(1)} %pad_maximum_fusion.1, bf16[64,2,8,128]{3,2,1,0:T(8,128)(2,1)S(1)} %get-tuple-element.37), kind=kOutput, calls=%fused_computation.68 | convolution fusion | flops 410519040 | bytes 8523776 | tf_op jit(solution)/shard_map/sub | solution.py:316
  53.8 3.6 %fusion.8 = bf16[2,512,1536]{2,1,0:T(8,128)(2,1)S(1)} fusion(f32[2,512,1536]{2,1,0:T(8,128)} %get-tuple-element.40, f32[2,512]{1,0:T(2,128)S(1)} %get-tuple-element.39), kind=kLoop, calls=%fused_computation.14 | loop fusion | flops 3145728 | bytes 9441280 | tf_op jit(solution)/shard_map/convert_element_type | solution.py:318
  57.5 1.2 convolution_convert_fusion.1
  59.4 47.1 %shard_map.101 = bf16[16,512,256]{2,1,0:T(8,128)(2,1)S(1)} custom-call(bf16[512,256]{1,0:T(8,128)(2,1)S(1)} %copy.122.own_ref), custom_call_target="tpu_custom_call" | custom-call | bytes 67108864 | tf_op jit(solution)/shard_map/pallas_call | solution.py:224
  106.5 3.2 %copy.100 = bf16[4,4,512,256]{3,1,2,0:T(4,128)(2,1)S(1)} copy(bf16[4,4,512,256]{3,2,1,0:T(8,128)(2,1)S(1)} %bitcast.99) | data formatting | bytes 8388608 | tf_op jit(solution)/shard_map/reshape | solution.py:322
  109.7 1.0 copy.131
  110.8 2.1 copy-done.2
  112.8 1.6 convolution_convert_fusion
  114.5 0.9 copy.101
  115.3 1.8 copy.95
  117.4 1.1 copy-done
  118.5 54.9 %shard_map.102 = (bf16[512,256]{1,0:T(8,128)(2,1)S(1)}, bf16[16,128,336]{2,1,0:T(8,128)(2,1)S(1)}) custom-call(bf16[4,512,384]{2,1,0:T(8,128)(2,1)S(1)} %pad.9.grad_ref, bf16[4,384,256]{2,1,0:T(8,128)(2,1)S(1)} %copy-done, bf16[16,128,336]{2,1,0:T(8,128)(2,1)S(1)} %bitcast.100), custom_call_target="tpu_custom_call" | custom-call | flops 1610612736 | bytes 67108864 | tf_op jit(solution)/shard_map/pallas_call | solution.py:224
  173.6 1.2 multiply_reduce_fusion
  174.8 2.6 %convolution_bitcast_fusion = f32[1536,128]{0,1:T(8,128)S(1)} fusion(bf16[2,512,128]{1,2,0:T(8,128)(2,1)} %bitcast.107, bf16[2,512,1536]{2,1,0:T(8,128)(2,1)} %copy-done.1), kind=kOutput, calls=%fused_computation.15 | convolution fusion | flops 402653184 | bytes 4194304 | tf_op jit(solution)/shard_map/hts,htd->sd/dot_general | solution.py:349
  177.5 3.6 %multiply_convert_fusion = bf16[2,512,1536]{2,1,0:T(8,128)(2,1)S(1)} fusion(bf16[2,512,128]{1,2,0:T(8,128)(2,1)S(1)} %bitcast.108, f32[2,512]{1,0:T(2,128)S(1)} %multiply_reduce_fusion, f32[2,512,1536]{2,1,0:T(8,128)} %get-tuple-element.40, f32[2,512]{1,0:T(2,128)S(1)} %get-tuple-element.39, bf16[1536,256]{1,0:T(8,128)(2,1)S(1)} %copy-done.4), kind=kOutput, calls=%fused_computation.1 | convolution fusion | flops 408944640 | bytes 10100736 | tf_op jit(solution)/shard_map/htd,sd->hts/dot_general | solution.py:345
  182.7 1.3 collective-permute-start.4
  184.0 1.5 collective-permute-start.5
  185.5 1.9 fusion.14
  187.4 1.0 concatenate.23
  188.4 0.9 copy.109
  189.3 1.0 constant_dynamic-slice_fusion
  190.2 2.3 copy.102
  192.5 1.5 collective-permute-start.3
  194.0 19.0 %collective-permute-done.5 = bf16[512,256]{0,1:T(8,128)(2,1)} collective-permute-done((bf16[512,256]{0,1:T(8,128)(2,1)}, bf16[512,256]{0,1:T(8,128)(2,1)}, u32[]{:S(2)}, u32[]{:S(2)}) %collective-permute-start.5) | collective-permute-done | bytes 262176 | tf_op jit(solution)/shard_map/ppermute | solution.py:18
  213.0 1.1 fusion.21
  214.3 1.8 pad_maximum_fusion.3
  216.0 4.2 %all-to-all-start.2 = ((bf16[4,128,512]{2,1,0:T(8,128)(2,1)}), bf16[4,128,512]{2,1,0:T(8,128)(2,1)S(1)}, u32[]{:S(2)}, u32[]{:S(2)}) async-start(bf16[4,128,512]{2,1,0:T(8,128)(2,1)} %pad_maximum_fusion.3), calls=%async_computation.2 | async-start | bytes 1048576 | tf_op jit(solution)/shard_map/all_to_all | solution.py:281
  220.3 5.3 %convolution_multiply_fusion = f32[336,1024]{1,0:T(8,128)} fusion(bf16[2048,1024]{1,0:T(8,128)(2,1)} %bitcast.104, bf16[128,16,336]{0,2,1:T(8,128)(2,1)} %all-to-all-done.1), kind=kOutput, calls=%fused_computation.23 | convolution fusion | flops 1409630208 | bytes 6946816 | tf_op jit(solution)/shard_map/dot_general | solution.py:27
  225.5 3.6 %all-to-all-done.2 = bf16[4,128,512]{2,1,0:T(8,128)(2,1)S(1)} async-done(((bf16[4,128,512]{2,1,0:T(8,128)(2,1)}), bf16[4,128,512]{2,1,0:T(8,128)(2,1)S(1)}, u32[]{:S(2)}, u32[]{:S(2)}) %all-to-all-start.2) | async-done | bytes 524320 | tf_op jit(solution)/shard_map/all_to_all | solution.py:281
  229.4 0.9 copy.114
  231.9 1.5 copy.103
  233.9 1.1 copy.113
  (54 shorter events, 6.8 us)
Async XLA Ops:
  0.6 8.2 %copy-start.11 = (bf16[128,2688]{1,0:T(8,128)(2,1)S(1)}, bf16[128,2688]{1,0:T(8,128)(2,1)}, u32[]{:S(2)}) copy-start(bf16[128,2688]{1,0:T(8,128)(2,1)} %param.9) | copy-start | bytes 2064388
  0.6 10.8 %copy-start.12 = (bf16[336,1024]{1,0:T(8,128)(2,1)S(1)}, bf16[336,1024]{1,0:T(8,128)(2,1)}, u32[]{:S(2)}) copy-start(bf16[336,1024]{1,0:T(8,128)(2,1)} %param.10) | copy-start | bytes 2064388
  0.7 10.9 %copy-start.13 = (s32[2048]{0:T(1024)S(1)}, s32[2048]{0:T(1024)}, u32[]{:S(2)}) copy-start(s32[2048]{0:T(1024)} %param.11) | copy-start | bytes 24580
  4.6 13.1 %all-to-all-start = ((bf16[128,4,512]{2,0,1:T(8,128)(2,1)}), bf16[128,4,512]{2,0,1:T(8,128)(2,1)S(1)}, u32[]{:S(2)}, u32[]{:S(2)}) async-start(bf16[128,4,512]{2,0,1:T(8,128)(2,1)} %pad_maximum_fusion.2), calls=%async_computation | async-start | bytes 1048576 | tf_op jit(solution)/shard_map/all_to_all | solution.py:278
  9.2 24.9 %collective-permute-start = (bf16[128,2688]{0,1:T(8,128)(2,1)S(1)}, bf16[128,2688]{0,1:T(8,128)(2,1)}, u32[]{:S(2)}, u32[]{:S(2)}) collective-permute-start(bf16[128,2688]{0,1:T(8,128)(2,1)S(1)} %copy.90), channel_id=1, source_target_pairs={{0,1},{1,0},{2,3},{3,2},{4,5},{5,4},{6,7},{7,6},{8,9},{9,8},{10,11... | collective-permute-start | bytes 2064392 | tf_op jit(solution)/shard_map/ppermute | solution.py:23
  17.8 30.3 %copy-start.9 = (bf16[64,2,8,128]{3,2,1,0:T(8,128)(2,1)}, bf16[64,2,8,128]{3,2,1,0:T(8,128)(2,1)S(1)}, u32[]{:S(2)}) copy-start(bf16[64,2,8,128]{3,2,1,0:T(8,128)(2,1)S(1)} %get-tuple-element.37) | copy-start | bytes 786436
  17.8 11.9 %collective-permute-start.1 = (bf16[512,256]{1,0:T(8,128)(2,1)S(1)}, bf16[512,256]{1,0:T(8,128)(2,1)S(1)}, u32[]{:S(2)}, u32[]{:S(2)}) collective-permute-start(bf16[512,256]{1,0:T(8,128)(2,1)S(1)} %get-tuple-element.38), channel_id=1, source_target_pairs={{0,16},{2,18},{4,20},{6,22},{8,24},{10,26},{12,28},{14,30},{1,17},... | collective-permute-start | bytes 786440 | tf_op jit(solution)/shard_map/ppermute | solution.py:18
  22.9 11.1 %collective-permute-start.2 = (bf16[512,256]{1,0:T(8,128)(2,1)S(1)}, bf16[512,256]{1,0:T(8,128)(2,1)S(1)}, u32[]{:S(2)}, u32[]{:S(2)}) collective-permute-start(bf16[512,256]{1,0:T(8,128)(2,1)S(1)} %get-tuple-element.38), channel_id=1, source_target_pairs={{0,8},{2,10},{4,12},{6,14},{8,16},{10,18},{12,20},{14,22},{16,24},... | collective-permute-start | bytes 786440 | tf_op jit(solution)/shard_map/ppermute | solution.py:18
  34.1 23.3 %copy-start.3 = (bf16[1536,256]{1,0:T(8,128)(2,1)}, bf16[1536,256]{1,0:T(8,128)(2,1)S(1)}, u32[]{:S(2)}) copy-start(bf16[1536,256]{1,0:T(8,128)(2,1)S(1)} %pad_maximum_fusion.1) | copy-start | bytes 2359300
  36.4 78.9 %all-to-all-start.1 = ((bf16[128,16,336]{0,2,1:T(8,128)(2,1)}), bf16[128,16,336]{0,2,1:T(8,128)(2,1)}, u32[]{:S(2)}, u32[]{:S(2)}) async-start(bf16[128,16,336]{0,2,1:T(8,128)(2,1)} %bitcast.3), calls=%async_computation.1 | async-start | bytes 2752512 | tf_op jit(solution)/shard_map/all_to_all | solution.py:300
  57.4 1.8 copy-start.1
  59.2 50.5 %copy-start.8 = (bf16[2,512,128]{1,2,0:T(8,128)(2,1)}, bf16[2,512,128]{1,2,0:T(8,128)(2,1)S(1)}, u32[]{:S(2)}) copy-start(bf16[2,512,128]{1,2,0:T(8,128)(2,1)S(1)} %convolution_convert_fusion.1) | copy-start | bytes 786436
  110.8 2.1 copy-start.2
  117.4 1.1 copy-start
  173.5 4.0 %copy-start.4 = (bf16[1536,256]{1,0:T(8,128)(2,1)S(1)}, bf16[1536,256]{1,0:T(8,128)(2,1)}, u32[]{:S(2)}) copy-start(bf16[1536,256]{1,0:T(8,128)(2,1)} %copy-done.3) | copy-start | bytes 2359300
  173.6 1.2 copy-start.6
  174.8 2.6 %copy-start.7 = (bf16[512,256]{0,1:T(8,128)(2,1)S(1)}, bf16[512,256]{0,1:T(8,128)(2,1)}, u32[]{:S(2)}) copy-start(bf16[512,256]{0,1:T(8,128)(2,1)} %copy-done.6) | copy-start | bytes 786436
  177.5 3.6 %copy-start.10 = (bf16[64,2,8,128]{3,2,1,0:T(8,128)(2,1)S(1)}, bf16[64,2,8,128]{3,2,1,0:T(8,128)(2,1)}, u32[]{:S(2)}) copy-start(bf16[64,2,8,128]{3,2,1,0:T(8,128)(2,1)} %copy-done.9) | copy-start | bytes 786436
  181.1 4.4 %copy-start.5 = (bf16[1536,256]{1,0:T(8,128)(2,1)S(1)}, bf16[1536,256]{1,0:T(8,128)(2,1)}, u32[]{:S(2)}) copy-start(bf16[1536,256]{1,0:T(8,128)(2,1)} %copy-done.3) | copy-start | bytes 2359300
  182.7 11.3 %collective-permute-start.4 = (bf16[512,256]{0,1:T(8,128)(2,1)}, bf16[512,256]{0,1:T(8,128)(2,1)}, u32[]{:S(2)}, u32[]{:S(2)}) collective-permute-start(bf16[512,256]{0,1:T(8,128)(2,1)} %get-tuple-element.33), channel_id=1, source_target_pairs={{8,0},{10,2},{12,4},{14,6},{16,8},{18,10},{20,12},{22,14},{24,16},... | collective-permute-start | bytes 786440 | tf_op jit(solution)/shard_map/ppermute | solution.py:18
  184.0 29.0 %collective-permute-start.5 = (bf16[512,256]{0,1:T(8,128)(2,1)}, bf16[512,256]{0,1:T(8,128)(2,1)}, u32[]{:S(2)}, u32[]{:S(2)}) collective-permute-start(bf16[512,256]{0,1:T(8,128)(2,1)} %get-tuple-element.34), channel_id=1, source_target_pairs={{16,0},{18,2},{20,4},{22,6},{24,8},{26,10},{28,12},{30,14},{17,1},... | collective-permute-start | bytes 786440 | tf_op jit(solution)/shard_map/ppermute | solution.py:18
  192.5 39.4 %collective-permute-start.3 = (bf16[8,128,336]{1,2,0:T(8,128)(2,1)}, bf16[8,128,336]{1,2,0:T(8,128)(2,1)}, u32[]{:S(2)}, u32[]{:S(2)}) collective-permute-start(bf16[8,128,336]{1,2,0:T(8,128)(2,1)} %copy.102), channel_id=1, source_target_pairs={{0,1},{1,0},{2,3},{3,2},{4,5},{5,4},{6,7},{7,6},{8,9},{9,8},{10,11... | collective-permute-start | bytes 2064392 | tf_op jit(solution)/shard_map/ppermute | solution.py:23
  216.0 13.1 %all-to-all-start.2 = ((bf16[4,128,512]{2,1,0:T(8,128)(2,1)}), bf16[4,128,512]{2,1,0:T(8,128)(2,1)S(1)}, u32[]{:S(2)}, u32[]{:S(2)}) async-start(bf16[4,128,512]{2,1,0:T(8,128)(2,1)} %pad_maximum_fusion.3), calls=%async_computation.2 | async-start | bytes 1048576 | tf_op jit(solution)/shard_map/all_to_all | solution.py:281
